TPU v7x, 256 devices: a whole 4x4x8 slice. The times are simulated.
256 devices in a mesh: long: 64 (over z_hi, y, x, core), short: 4 (over z_lo).
Axes of the slice: x: 4, y: 4, z: 8 (z_hi: 2, z_lo: 4; z = z_hi * 4 + z_lo), core: 2. Of those that a mesh axis runs over, the one named last changes fastest.
Arguments:
- field: bfloat16 [64, 1024, 1024], P(None, 'long', 'short'), may hold values from -6 to 6
- cotangent: bfloat16 [64, 1024, 1024], P(None, 'long', 'short'), may hold values from -6 to 6
- first_filter: bfloat16 [9, 64, 64], replicated, may hold values from -0.25 to 0.25
- second_filter: bfloat16 [9, 64, 64], replicated, may hold values from -0.25 to 0.25
Outputs:
- grad_field: bfloat16 [64, 1024, 1024], P(None, 'long', 'short')
- grad_first: float32 [9, 64, 64], replicated
- grad_second: float32 [9, 64, 64], replicated
All inputs are finite; a program needn't handle non-finite values.
Results may differ from a plain program's by a relative error of at most 0.0095.
Values may be sent and summed in bfloat16 or wider, within the bound.
A program may use at most 64 MiB of HBM per device.

v0:
```python
import math

import jax
import jax.numpy as jnp
from jax import lax
from jax.sharding import PartitionSpec as P


def with_halo(block, sides, width):
    for axis, dim in sides:
        count = lax.axis_size(axis)
        forward = [(i, i + 1) for i in range(count - 1)]
        backward = [(target, source) for source, target in forward]
        low = lax.ppermute(
            lax.slice_in_dim(block, block.shape[dim] - width, None, axis=dim), axis, forward
        )
        high = lax.ppermute(lax.slice_in_dim(block, 0, width, axis=dim), axis, backward)
        block = jnp.concatenate([low, block, high], axis=dim)
    return block


def dilated(padded, taps, dilation):
    width = taps.shape[1]
    kernel = taps.reshape(3, 3, width, width).transpose(2, 3, 0, 1)
    result = lax.conv_general_dilated(
        padded[None],
        kernel,
        (1, 1),
        "VALID",
        rhs_dilation=(dilation, dilation),
        preferred_element_type=jnp.float32,
    )
    return result[0]


def flipped(taps):
    return taps[::-1].transpose(0, 2, 1)


def correlate(grad, padded, dilation):
    height = grad.shape[1]
    breadth = grad.shape[2]
    terms = []
    for row_tap in range(3):
        for col_tap in range(3):
            window = padded[
                :,
                row_tap * dilation : row_tap * dilation + height,
                col_tap * dilation : col_tap * dilation + breadth,
            ]
            terms.append(
                jnp.einsum("orc,irc->oi", grad, window, preferred_element_type=jnp.float32)
            )
    return jnp.stack(terms)


def shards(field, cotangent, first_filter, second_filter):
    tile_rows = field.shape[1]
    tile_cols = field.shape[2]
    total_rows = tile_rows * lax.axis_size("long")
    total_cols = tile_cols * lax.axis_size("short")
    grad_scale = 1.0 / math.sqrt(total_rows * total_cols)
    field_wide = with_halo(field, (("long", 1), ("short", 2)), 4)
    act_first = jnp.maximum(field_wide, 0)
    hidden = (field.astype(jnp.float32) + dilated(act_first, first_filter, 4)).astype(jnp.bfloat16)
    act_second = with_halo(jnp.maximum(hidden, 0), (("long", 1), ("short", 2)), 8)
    grad_wide = with_halo(cotangent, (("long", 1), ("short", 2)), 8)
    upstream = dilated(grad_wide, flipped(second_filter), 8)
    grad_hidden = (cotangent.astype(jnp.float32) + jnp.where(hidden > 0, upstream, 0.0)).astype(
        jnp.bfloat16
    )
    hidden_grad_wide = with_halo(grad_hidden, (("long", 1), ("short", 2)), 4)
    back_term = dilated(hidden_grad_wide, flipped(first_filter), 4)
    grad_field = (grad_hidden.astype(jnp.float32) + jnp.where(field > 0, back_term, 0.0)).astype(
        jnp.bfloat16
    )
    local_second = correlate(cotangent, act_second, 8) * grad_scale
    local_first = correlate(grad_hidden, act_first, 4) * grad_scale
    grad_first, grad_second = lax.psum((local_first, local_second), ("long", "short"))
    return (grad_field, grad_first, grad_second)


def solution(mesh):
    in_specs = (P(None, "long", "short"), P(None, "long", "short"), P(), P())
    out_specs = (P(None, "long", "short"), P(), P())
    return jax.shard_map(shards, mesh=mesh, in_specs=in_specs, out_specs=out_specs, check_vma=False)
```

profile of v0, /device:TPU:1, one launch (start us, length us, event | category | flops | bytes accessed | tf_op | source)
XLA Modules:
  0.0 416.7 jit_solution(7213138220916043682)
XLA Ops:
  8.4 4.5 %collective-permute-start = (bf16[64,4,256]{2,0,1:T(8,128)(2,1)S(1)}, bf16[64,4,256]{2,0,1:T(8,128)(2,1)S(1)}, u32[]{:S(2)}, u32[]{:S(2)}) collective-permute-start(bf16[64,4,256]{2,0,1:T(8,128)(2,1)S(1)} %copy.117), channel_id=1, source_target_pairs={{0,4},{4,8},{8,12},{12,16},{16,20},{20,24},{24,28},{28,32},{32,36}... | collective-permute-start | bytes 393224 | tf_op jit(solution)/shard_map/ppermute | solution.py:14
  13.0 1.9 collective-permute-start.1
  14.9 2.6 copy.42
  19.5 3.6 collective-permute-start.2
  25.4 2.4 collective-permute-start.4
  27.9 2.7 collective-permute-start.5
  34.3 1.9 maximum_maximum_fusion.1
  36.2 2.9 copy.37
  40.0 2.8 fusion.31
  43.4 2.0 copy.92
  47.9 5.7 %collective-permute-start.12 = (bf16[64,8,256]{2,0,1:T(8,128)(2,1)}, bf16[64,8,256]{2,0,1:T(8,128)(2,1)}, u32[]{:S(2)}, u32[]{:S(2)}) collective-permute-start(bf16[64,8,256]{2,0,1:T(8,128)(2,1)} %get-tuple-element.25), channel_id=1, source_target_pairs={{0,4},{4,8},{8,12},{12,16},{16,20},{20,24},{24,28},{28,32},{32,36}... | collective-permute-start | bytes 786440 | tf_op jit(solution)/shard_map/ppermute | solution.py:14
  56.4 3.5 collective-permute-start.6
  63.3 3.3 collective-permute-done.6
  66.6 3.4 pad_maximum_fusion
  71.8 2.0 fusion.25
  76.0 2.6 copy.93
  79.0 3.5 collective-permute-start.8
  89.7 4.8 %collective-permute-start.10 = (bf16[64,24,4]{2,0,1:T(8,128)(2,1)S(1)}, bf16[64,24,4]{2,0,1:T(8,128)(2,1)S(1)}, u32[]{:S(2)}, u32[]{:S(2)}) collective-permute-start(bf16[64,24,4]{2,0,1:T(8,128)(2,1)S(1)} %get-tuple-element.21), channel_id=1, source_target_pairs={{0,1},{1,2},{2,3},{4,5},{5,6},{6,7},{8,9},{9,10},{10,11},{12,13},{... | collective-permute-start | bytes 36872 | tf_op jit(solution)/shard_map/ppermute | solution.py:14
  98.4 5.4 %collective-permute-start.14 = (bf16[64,32,8]{2,0,1:T(8,128)(2,1)}, bf16[64,32,8]{2,0,1:T(8,128)(2,1)}, u32[]{:S(2)}, u32[]{:S(2)}) collective-permute-start(bf16[64,32,8]{2,0,1:T(8,128)(2,1)} %get-tuple-element.18), channel_id=1, source_target_pairs={{0,1},{1,2},{2,3},{4,5},{5,6},{6,7},{8,9},{9,10},{10,11},{12,13},{... | collective-permute-start | bytes 98312 | tf_op jit(solution)/shard_map/ppermute | solution.py:14
  103.8 3.6 collective-permute-done.11
  109.2 2.9 copy.50
  116.7 2.5 copy.94
  119.3 2.5 pad_maximum_fusion.1
  128.4 278.1 %all-reduce.3.cloned.1.call-done = (f32[9,64,64]{2,1,0:T(8,128)}, f32[9,64,64]{2,1,0:T(8,128)}) async-done(((f32[9,64,64]{2,1,0:T(8,128)}, f32[9,64,64]{2,1,0:T(8,128)}), (f32[9,64,64]{2,1,0:T(8,128)}, f32[9,64,64]{2,1,0:T(8,128)})) %all-reduce.3.cloned.1.call-update) | async-done | bytes 294928 | tf_op jit(solution)/shard_map/psum | solution.py:79
  (118 shorter events, 50.7 us)
Async XLA Ops:
  7.2 10.4 %copy-start.2 = (bf16[64,16,256]{2,1,0:T(8,128)(2,1)S(1)}, bf16[64,16,256]{2,1,0:T(8,128)(2,1)}, u32[]{:S(2)}) copy-start(bf16[64,16,256]{2,1,0:T(8,128)(2,1)} %param.4) | copy-start | bytes 1572868
  7.2 399.3 %all-reduce.3.cloned.1.call-start = ((), (), s32[]{:S(2)}) async-start(), calls=%async_computation | async-start | bytes 1179648 | tf_op jit(solution)/shard_map/psum | solution.py:79
  8.4 9.1 %collective-permute-start = (bf16[64,4,256]{2,0,1:T(8,128)(2,1)S(1)}, bf16[64,4,256]{2,0,1:T(8,128)(2,1)S(1)}, u32[]{:S(2)}, u32[]{:S(2)}) collective-permute-start(bf16[64,4,256]{2,0,1:T(8,128)(2,1)S(1)} %copy.117), channel_id=1, source_target_pairs={{0,4},{4,8},{8,12},{12,16},{16,20},{20,24},{24,28},{28,32},{32,36}... | collective-permute-start | bytes 393224 | tf_op jit(solution)/shard_map/ppermute | solution.py:14
  13.0 6.3 %collective-permute-start.1 = (bf16[64,4,256]{2,0,1:T(8,128)(2,1)S(1)}, bf16[64,4,256]{2,0,1:T(8,128)(2,1)S(1)}, u32[]{:S(2)}, u32[]{:S(2)}) collective-permute-start(bf16[64,4,256]{2,0,1:T(8,128)(2,1)S(1)} %copy.118), channel_id=1, source_target_pairs={{4,0},{8,4},{12,8},{16,12},{20,16},{24,20},{28,24},{32,28},{36,32}... | collective-permute-start | bytes 393224 | tf_op jit(solution)/shard_map/ppermute | solution.py:17
  17.8 12.8 %copy-start.13 = (bf16[9,64,64]{2,1,0:T(8,128)(2,1)S(1)}, bf16[9,64,64]{2,1,0:T(8,128)(2,1)}, u32[]{:S(2)}) copy-start(bf16[9,64,64]{2,1,0:T(8,128)(2,1)} %param.7) | copy-start | bytes 221188
  19.3 16.9 %copy-start = (bf16[64,24,256]{2,0,1:T(8,128)(2,1)}, bf16[64,24,256]{2,0,1:T(8,128)(2,1)S(1)}, u32[]{:S(2)}) copy-start(bf16[64,24,256]{2,0,1:T(8,128)(2,1)S(1)} %constant_dynamic-update-slice_fusion) | copy-start | bytes 2359300
  19.5 13.3 %collective-permute-start.2 = (bf16[64,24,4]{2,0,1:T(8,128)(2,1)S(1)}, bf16[64,24,4]{2,0,1:T(8,128)(2,1)S(1)}, u32[]{:S(2)}, u32[]{:S(2)}) collective-permute-start(bf16[64,24,4]{2,0,1:T(8,128)(2,1)S(1)} %get-tuple-element.23), channel_id=1, source_target_pairs={{0,1},{1,2},{2,3},{4,5},{5,6},{6,7},{8,9},{9,10},{10,11},{12,13},{... | collective-permute-start | bytes 36872 | tf_op jit(solution)/shard_map/ppermute | solution.py:14
  23.1 10.4 %collective-permute-start.3 = (bf16[64,24,4]{2,0,1:T(8,128)(2,1)S(1)}, bf16[64,24,4]{2,0,1:T(8,128)(2,1)S(1)}, u32[]{:S(2)}, u32[]{:S(2)}) collective-permute-start(bf16[64,24,4]{2,0,1:T(8,128)(2,1)S(1)} %get-tuple-element.24), channel_id=1, source_target_pairs={{1,0},{2,1},{3,2},{5,4},{6,5},{7,6},{9,8},{10,9},{11,10},{13,12},{... | collective-permute-start | bytes 36872 | tf_op jit(solution)/shard_map/ppermute | solution.py:17
  25.4 30.1 %collective-permute-start.4 = (bf16[64,8,256]{0,1,2:T(8,128)(2,1)}, bf16[64,8,256]{0,1,2:T(8,128)(2,1)}, u32[]{:S(2)}, u32[]{:S(2)}) collective-permute-start(bf16[64,8,256]{0,1,2:T(8,128)(2,1)} %get-tuple-element.19), channel_id=1, source_target_pairs={{0,4},{4,8},{8,12},{12,16},{16,20},{20,24},{24,28},{28,32},{32,36}... | collective-permute-start | bytes 786440 | tf_op jit(solution)/shard_map/ppermute | solution.py:14
  27.9 27.7 %collective-permute-start.5 = (bf16[64,8,256]{0,1,2:T(8,128)(2,1)}, bf16[64,8,256]{0,1,2:T(8,128)(2,1)}, u32[]{:S(2)}, u32[]{:S(2)}) collective-permute-start(bf16[64,8,256]{0,1,2:T(8,128)(2,1)} %get-tuple-element.20), channel_id=1, source_target_pairs={{4,0},{8,4},{12,8},{16,12},{20,16},{24,20},{28,24},{32,28},{36,32}... | collective-permute-start | bytes 786440 | tf_op jit(solution)/shard_map/ppermute | solution.py:17
  47.0 31.6 %copy-start.6 = (bf16[64,16,256]{2,0,1:T(8,128)(2,1)}, bf16[64,16,256]{2,0,1:T(8,128)(2,1)S(1)}, u32[]{:S(2)}) copy-start(bf16[64,16,256]{2,0,1:T(8,128)(2,1)S(1)} %get-tuple-element.12) | copy-start | bytes 1572868
  47.0 14.3 %copy-start.1 = (bf16[64,24,256]{2,0,1:T(8,128)(2,1)S(1)}, bf16[64,24,256]{2,0,1:T(8,128)(2,1)}, u32[]{:S(2)}) copy-start(bf16[64,24,256]{2,0,1:T(8,128)(2,1)} %copy-done) | copy-start | bytes 2359300
  47.0 14.3 %copy-start.9 = (bf16[64,24,4]{2,0,1:T(8,128)(2,1)S(1)}, bf16[64,24,4]{2,0,1:T(8,128)(2,1)}, u32[]{:S(2)}) copy-start(bf16[64,24,4]{2,0,1:T(8,128)(2,1)} %copy-done.8) | copy-start | bytes 36868
  47.0 14.3 %copy-start.11 = (bf16[64,24,4]{2,0,1:T(8,128)(2,1)S(1)}, bf16[64,24,4]{2,0,1:T(8,128)(2,1)}, u32[]{:S(2)}) copy-start(bf16[64,24,4]{2,0,1:T(8,128)(2,1)} %copy-done.10) | copy-start | bytes 36868
  47.9 40.4 %collective-permute-start.12 = (bf16[64,8,256]{2,0,1:T(8,128)(2,1)}, bf16[64,8,256]{2,0,1:T(8,128)(2,1)}, u32[]{:S(2)}, u32[]{:S(2)}) collective-permute-start(bf16[64,8,256]{2,0,1:T(8,128)(2,1)} %get-tuple-element.25), channel_id=1, source_target_pairs={{0,4},{4,8},{8,12},{12,16},{16,20},{20,24},{24,28},{28,32},{32,36}... | collective-permute-start | bytes 786440 | tf_op jit(solution)/shard_map/ppermute | solution.py:14
  53.6 34.6 %collective-permute-start.13 = (bf16[64,8,256]{2,0,1:T(8,128)(2,1)}, bf16[64,8,256]{2,0,1:T(8,128)(2,1)S(1)}, u32[]{:S(2)}, u32[]{:S(2)}) collective-permute-start(bf16[64,8,256]{2,0,1:T(8,128)(2,1)} %get-tuple-element.26), channel_id=1, source_target_pairs={{4,0},{8,4},{12,8},{16,12},{20,16},{24,20},{28,24},{32,28},{36,32}... | collective-permute-start | bytes 786440 | tf_op jit(solution)/shard_map/ppermute | solution.py:17
  56.4 10.2 %collective-permute-start.6 = (bf16[64,32,8]{0,1,2:T(8,128)(2,1)S(1)}, bf16[64,32,8]{0,1,2:T(8,128)(2,1)S(1)}, u32[]{:S(2)}, u32[]{:S(2)}) collective-permute-start(bf16[64,32,8]{0,1,2:T(8,128)(2,1)S(1)} %get-tuple-element.13), channel_id=1, source_target_pairs={{0,1},{1,2},{2,3},{4,5},{5,6},{6,7},{8,9},{9,10},{10,11},{12,13},{... | collective-permute-start | bytes 98312 | tf_op jit(solution)/shard_map/ppermute | solution.py:14
  59.9 6.7 %collective-permute-start.7 = (bf16[64,32,8]{0,1,2:T(8,128)(2,1)S(1)}, bf16[64,32,8]{0,1,2:T(8,128)(2,1)S(1)}, u32[]{:S(2)}, u32[]{:S(2)}) collective-permute-start(bf16[64,32,8]{0,1,2:T(8,128)(2,1)S(1)} %get-tuple-element.14), channel_id=1, source_target_pairs={{1,0},{2,1},{3,2},{5,4},{6,5},{7,6},{9,8},{10,9},{11,10},{13,12},{... | collective-permute-start | bytes 98312 | tf_op jit(solution)/shard_map/ppermute | solution.py:17
  79.0 10.3 %collective-permute-start.8 = (bf16[64,4,256]{2,0,1:T(8,128)(2,1)S(1)}, bf16[64,4,256]{2,0,1:T(8,128)(2,1)S(1)}, u32[]{:S(2)}, u32[]{:S(2)}) collective-permute-start(bf16[64,4,256]{2,0,1:T(8,128)(2,1)S(1)} %get-tuple-element.27), channel_id=1, source_target_pairs={{0,4},{4,8},{8,12},{12,16},{16,20},{20,24},{24,28},{28,32},{32,36}... | collective-permute-start | bytes 393224 | tf_op jit(solution)/shard_map/ppermute | solution.py:14
  82.5 6.9 %collective-permute-start.9 = (bf16[64,4,256]{2,0,1:T(8,128)(2,1)S(1)}, bf16[64,4,256]{2,0,1:T(8,128)(2,1)S(1)}, u32[]{:S(2)}, u32[]{:S(2)}) collective-permute-start(bf16[64,4,256]{2,0,1:T(8,128)(2,1)S(1)} %get-tuple-element.28), channel_id=1, source_target_pairs={{4,0},{8,4},{12,8},{16,12},{20,16},{24,20},{28,24},{32,28},{36,32}... | collective-permute-start | bytes 393224 | tf_op jit(solution)/shard_map/ppermute | solution.py:17
  89.7 14.1 %collective-permute-start.10 = (bf16[64,24,4]{2,0,1:T(8,128)(2,1)S(1)}, bf16[64,24,4]{2,0,1:T(8,128)(2,1)S(1)}, u32[]{:S(2)}, u32[]{:S(2)}) collective-permute-start(bf16[64,24,4]{2,0,1:T(8,128)(2,1)S(1)} %get-tuple-element.21), channel_id=1, source_target_pairs={{0,1},{1,2},{2,3},{4,5},{5,6},{6,7},{8,9},{9,10},{10,11},{12,13},{... | collective-permute-start | bytes 36872 | tf_op jit(solution)/shard_map/ppermute | solution.py:14
  94.5 12.9 %collective-permute-start.11 = (bf16[64,24,4]{2,0,1:T(8,128)(2,1)S(1)}, bf16[64,24,4]{2,0,1:T(8,128)(2,1)S(1)}, u32[]{:S(2)}, u32[]{:S(2)}) collective-permute-start(bf16[64,24,4]{2,0,1:T(8,128)(2,1)S(1)} %get-tuple-element.22), channel_id=1, source_target_pairs={{1,0},{2,1},{3,2},{5,4},{6,5},{7,6},{9,8},{10,9},{11,10},{13,12},{... | collective-permute-start | bytes 36872 | tf_op jit(solution)/shard_map/ppermute | solution.py:17
  97.1 22.2 %collective-permute-start.15 = (bf16[64,32,8]{2,0,1:T(8,128)(2,1)}, bf16[64,32,8]{2,0,1:T(8,128)(2,1)}, u32[]{:S(2)}, u32[]{:S(2)}) collective-permute-start(bf16[64,32,8]{2,0,1:T(8,128)(2,1)} %get-tuple-element.17), channel_id=1, source_target_pairs={{1,0},{2,1},{3,2},{5,4},{6,5},{7,6},{9,8},{10,9},{11,10},{13,12},{... | collective-permute-start | bytes 98312 | tf_op jit(solution)/shard_map/ppermute | solution.py:17
  98.4 20.9 %collective-permute-start.14 = (bf16[64,32,8]{2,0,1:T(8,128)(2,1)}, bf16[64,32,8]{2,0,1:T(8,128)(2,1)}, u32[]{:S(2)}, u32[]{:S(2)}) collective-permute-start(bf16[64,32,8]{2,0,1:T(8,128)(2,1)} %get-tuple-element.18), channel_id=1, source_target_pairs={{0,1},{1,2},{2,3},{4,5},{5,6},{6,7},{8,9},{9,10},{10,11},{12,13},{... | collective-permute-start | bytes 98312 | tf_op jit(solution)/shard_map/ppermute | solution.py:14
  (12 other events, 21.0 us)
Sparse Core Ops, SparseCore 0:
  127.1 279.3 all-reduce.2
where the time goes:
time: 418 us; the launch traced here: 417 us
  waiting for transfers between devices  287 us (69%)
  starting transfers between devices  47.3 us (11%)
  local copies, waits for them, and re-layouts  36.2 us (9%)
  other arithmetic  17.2 us (4%)
  between operations  14.8 us (4%)
  matrix products  14 us (3%)
    psum x1, waiting for transfers between devices, shards(): lax.psum((local_first, local_second), ('long', 'short'))  278 us
    ppermute x8, starting transfers between devices, with_halo(): lax.ppermute(lax.slice_in_dim(block, block.shape[dim] - width, None, axis...  33.5 us
    unnamed x49, local copies, waits for them, and re-layouts  16.4 us
    ppermute x8, starting transfers between devices, with_halo(): lax.ppermute(lax.slice_in_dim(block, 0, width, axis=dim), axis, backward)  13.8 us
    concatenate x5, other arithmetic, with_halo(): block = jnp.concatenate([low, block, high], axis=dim)  8.86 us
  transfers between devices with their start and end apart: 17, of which 5 were waited for; matrix products, arithmetic and copies ran while one was open for 13% of the time, Pallas kernels for 0%

commit v1 on v0

v1 whole, which is shorter than its diff:
```python
import math

import jax
import jax.numpy as jnp
from jax import lax
from jax.experimental import pallas as pl
from jax.experimental.pallas import tpu as pltpu
from jax.sharding import PartitionSpec as P

BF = jnp.bfloat16
F32 = jnp.float32
MESH = pl.DeviceIdType.MESH
CH, TR, TC = 64, 16, 256
K = 9 * CH
LONG, SHORT = 64, 4
PLANE = 32
NZ = LONG // PLANE * SHORT
CHUNK = 32
NCHUNK = K // CHUNK
OWNERS = tuple(range(0, 32, 2)) + (1, 21)

ROWS = ((-1, 0), (1, 0))
PACKS = ((0, -1), (0, 1), (-1, -1), (-1, 1), (1, -1), (1, 1))


def nt_dot(a, b):
    return lax.dot_general(a, b, (((1,), (1,)), ((), ())), preferred_element_type=F32)


def dot(a, b):
    return jnp.dot(a, b, preferred_element_type=F32)


def kernel(scale, field_hbm, cot_hbm, w1_ref, w2_ref, gf_ref, gr_ref,
           raw_f, raw_c, xf, a2, fs, cs, gs, ps, pleft, pright, gps, gleft, gright,
           w1c, w1t, w2t, acc2, acc1, gb, ra, rb, fin, in_sem,
           h_send, h_recv, g_send, g_recv, a_send, a_recv, b_send, b_recv, c_send, c_recv):
    l = lax.axis_index("long")
    s = lax.axis_index("short")
    place = lax.rem(l, PLANE)
    base = l - place
    z = lax.div(l, PLANE) * SHORT + s

    in_f = pltpu.make_async_copy(field_hbm, raw_f, in_sem.at[0])
    in_c = pltpu.make_async_copy(cot_hbm, raw_c, in_sem.at[1])
    in_f.start()
    in_c.start()

    barrier = pltpu.get_barrier_semaphore()

    def greet(dev_l, dev_s):
        pl.semaphore_signal(barrier, inc=1, device_id=(dev_l, dev_s), device_id_type=MESH)

    for dl, ds in ROWS + PACKS:
        greet(lax.rem(l + dl + LONG, LONG), lax.rem(s + ds + SHORT, SHORT))

    @pl.loop(1, PLANE)
    def _(k):
        greet(base + lax.rem(place + k, PLANE), s)

    def z_peer(k):
        other = lax.rem(z + k, NZ)
        return lax.div(other, SHORT) * PLANE + place, lax.rem(other, SHORT)

    for k in range(1, NZ):
        greet(*z_peer(k))

    def there(dl, ds):
        ok = None
        for d, at, n in ((dl, l, LONG), (ds, s, SHORT)):
            if d == 0:
                continue
            here = at + d >= 0 if d < 0 else at + d < n
            ok = here if ok is None else jnp.logical_and(ok, here)
        return ok

    def exchange(messages, send_sems, recv_sems):
        copies = []
        for i, (dl, ds, src, dst) in enumerate(messages):
            copies.append(pltpu.make_async_remote_copy(
                src_ref=src, dst_ref=dst, send_sem=send_sems.at[i], recv_sem=recv_sems.at[i],
                device_id=(l + dl, s + ds), device_id_type=MESH))

        def start(i):
            dl, ds = messages[i][:2]
            pl.when(there(dl, ds))(lambda: copies[i].start())

        def wait_recv(i):
            dl, ds, _, dst = messages[i]
            from_there = there(-dl, -ds)
            pl.when(from_there)(lambda: copies[i].wait_recv())

            @pl.when(jnp.logical_not(from_there))
            def _():
                dst[...] = jnp.zeros(dst.shape, dst.dtype)

        def wait_send(i):
            dl, ds = messages[i][:2]
            pl.when(there(dl, ds))(lambda: copies[i].wait_send())

        return start, wait_recv, wait_send

    halo = [
        (-1, 0, fs.at[1, pl.ds(4, 4)], fs.at[1, pl.ds(20, 4)]),
        (1, 0, fs.at[1, pl.ds(16, 4)], fs.at[1, pl.ds(0, 4)]),
        (-1, 0, cs.at[1, pl.ds(8, 8)], cs.at[1, pl.ds(24, 8)]),
        (1, 0, cs.at[1, pl.ds(16, 8)], cs.at[1, pl.ds(0, 8)]),
        (0, -1, ps.at[0], pright.at[pl.ds(1, 2)]),
        (0, 1, ps.at[1], pleft.at[pl.ds(1, 2)]),
        (-1, -1, ps.at[0, pl.ds(0, 1)], pright.at[pl.ds(3, 1)]),
        (-1, 1, ps.at[1, pl.ds(0, 1)], pleft.at[pl.ds(3, 1)]),
        (1, -1, ps.at[0, pl.ds(1, 1)], pright.at[pl.ds(0, 1)]),
        (1, 1, ps.at[1, pl.ds(1, 1)], pleft.at[pl.ds(0, 1)]),
    ]
    h_start, h_wait, h_sent = exchange(halo, h_send, h_recv)
    ghalo = [
        (-1, 0, gs.at[1, pl.ds(4, 4)], gs.at[1, pl.ds(20, 4)]),
        (1, 0, gs.at[1, pl.ds(16, 4)], gs.at[1, pl.ds(0, 4)]),
        (0, -1, gps.at[0], gright.at[1]),
        (0, 1, gps.at[1], gleft.at[1]),
        (-1, -1, gps.at[0], gright.at[2]),
        (-1, 1, gps.at[1], gleft.at[2]),
        (1, -1, gps.at[0], gright.at[0]),
        (1, 1, gps.at[1], gleft.at[0]),
    ]
    g_start, g_wait, g_sent = exchange(ghalo, g_send, g_recv)

    for t in range(9):
        w1c[:, CH * t:CH * (t + 1)] = w1_ref[t]
    w1t[...] = w1_ref[...].reshape(K, CH).T
    w2t[...] = w2_ref[...].reshape(K, CH).T

    in_f.wait()
    own_f = jnp.swapaxes(raw_f[...], 0, 1)
    xf[...] = own_f
    fs[1, 4:20] = jnp.maximum(own_f, 0)
    in_c.wait()
    cs[1, 8:24] = jnp.swapaxes(raw_c[...], 0, 1)

    pl.semaphore_wait(barrier, len(ROWS + PACKS) + PLANE - 1 + NZ - 1)
    for i in range(4):
        h_start(i)
    for half in range(2):
        for side in range(2):
            c8 = 0 if side == 0 else TC - 8
            c4 = 0 if side == 0 else TC - 4
            pieces = [cs[1, 8 + 8 * half + k][:, c8:c8 + 8] for k in range(8)]
            pieces += [fs[1, 4 + 8 * half + k][:, c4:c4 + 4] for k in range(8)]
            pieces += [jnp.zeros((CH, 32), BF)]
            ps[side, half] = jnp.concatenate(pieces, axis=1)
    for i in range(4, 10):
        h_start(i)

    def shift_left(x, h, at, d):
        return jnp.concatenate([x[:, d:], h[:, at:at + d]], axis=1)

    def shift_right(x, h, at, d):
        return jnp.concatenate([h[:, at:at + d], x[:, :TC - d]], axis=1)

    def f_row(blk, k):
        e = 8 * blk + k - 4
        x = fs[1, e]
        fs[0, e] = shift_right(x, pleft[blk], 64 + 4 * k, 4)
        fs[2, e] = shift_left(x, pright[blk], 64 + 4 * k, 4)

    def c_row(blk, k):
        e = 8 * blk + k
        x = cs[1, e]
        cs[2, e] = shift_right(x, pleft[blk], 8 * k, 8)
        cs[0, e] = shift_left(x, pright[blk], 8 * k, 8)

    h_wait(4)
    h_wait(5)

    @pl.loop(1, 3)
    def _(blk):
        for k in range(8):
            f_row(blk, k)
            c_row(blk, k)

    for i in (6, 7, 8, 9, 0, 1):
        h_wait(i)
    for k in range(4):
        f_row(0, k + 4)
        f_row(3, k)

    def taps(ref, r, first, step):
        return jnp.concatenate([ref[b, r + first + step * a] for a in range(3) for b in range(3)], axis=0)

    @pl.loop(0, TR // 4)
    def _(g):
        for k in range(4):
            r = 4 * g + k
            h = xf[r].astype(F32) + dot(w1c[...], taps(fs, r, 0, 4))
            a2[r] = jnp.maximum(h.astype(BF), 0)

    h_wait(2)
    h_wait(3)

    @pl.loop(0, 2)
    def _(i):
        for k in range(8):
            c_row(3 * i, k)

    @pl.loop(0, TR // 4)
    def _(g):
        for k in range(4):
            r = 4 * g + k
            up = dot(w2t[...], taps(cs, r, 16, -8))
            gh = cs[1, r + 8].astype(F32) + jnp.where(a2[r].astype(F32) > 0, up, 0.0)
            gs[1, r + 4] = gh.astype(BF)

    g_start(0)
    g_start(1)
    for side in range(2):
        c4 = 0 if side == 0 else TC - 4
        pieces = [gs[1, 4 + k][:, c4:c4 + 4] for k in range(16)] + [jnp.zeros((CH, 64), BF)]
        gps[side] = jnp.concatenate(pieces, axis=1)
    for i in range(2, 8):
        g_start(i)

    acc2[...] = jnp.zeros_like(acc2)
    acc1[...] = jnp.zeros_like(acc1)

    @pl.loop(0, TR // 4)
    def _(g):
        r0 = 4 * g
        u2 = jnp.concatenate([taps(cs, r0 + k, 16, -8) for k in range(4)], axis=1)
        v2 = jnp.concatenate([a2[r0 + k] for k in range(4)], axis=1)
        acc2[...] += nt_dot(u2, v2)
        u1 = jnp.concatenate([taps(fs, r0 + k, 0, 4) for k in range(4)], axis=1)
        v1 = jnp.concatenate([gs[1, r0 + 4 + k] for k in range(4)], axis=1)
        acc1[...] += nt_dot(v1, u1)

    for t in range(9):
        gb[CH * t:CH * (t + 1), :] = jnp.concatenate(
            [acc2[CH * t:CH * (t + 1), :], acc1[:, CH * t:CH * (t + 1)]], axis=1).astype(BF)

    def a_copy(j):
        owner = OWNERS[j]
        slot = lax.rem(place - owner + PLANE - 1, PLANE)
        return pltpu.make_async_remote_copy(
            src_ref=gb.at[pl.ds(CHUNK * j, CHUNK)], dst_ref=ra.at[slot],
            send_sem=a_send.at[j], recv_sem=a_recv,
            device_id=(base + owner, s), device_id_type=MESH)

    for j in range(NCHUNK):
        pl.when(place != OWNERS[j])(lambda j=j: a_copy(j).start())

    for i in range(8):
        g_wait(i)

    def g_row(blk, e, at):
        x = gs[1, e]
        gs[2, e] = shift_right(x, gleft[blk], at, 4)
        gs[0, e] = shift_left(x, gright[blk], at, 4)

    for k in range(16):
        g_row(1, 4 + k, 4 * k)
    for k in range(4):
        g_row(0, k, 4 * (12 + k))
        g_row(2, 20 + k, 4 * k)

    @pl.loop(0, TR // 4)
    def _(g):
        for k in range(4):
            r = 4 * g + k
            back = dot(w1t[...], taps(gs, r, 8, -4))
            out = gs[1, r + 4].astype(F32) + jnp.where(xf[r].astype(F32) > 0, back, 0.0)
            gf_ref[r] = out.astype(BF)

    is_owner = jnp.logical_or(lax.rem(place, 2) == 0, jnp.logical_or(place == 1, place == 21))
    mine = jnp.where(place == 1, 16, jnp.where(place == 21, 17, lax.div(place, 2)))
    my_rows = pl.ds(pl.multiple_of(CHUNK * mine, CHUNK), CHUNK)

    def b_copy(k):
        return pltpu.make_async_remote_copy(
            src_ref=rb.at[0], dst_ref=rb.at[k], send_sem=b_send.at[k - 1], recv_sem=b_recv.at[k - 1],
            device_id=z_peer(k), device_id_type=MESH)

    def c_copy(k):
        return pltpu.make_async_remote_copy(
            src_ref=fin.at[my_rows], dst_ref=fin.at[my_rows], send_sem=c_send.at[k - 1],
            recv_sem=c_recv.at[mine], device_id=(base + lax.rem(place + k, PLANE), s),
            device_id_type=MESH)

    @pl.when(is_owner)
    def _():
        pltpu.make_async_copy(ra, ra, a_recv).wait()
        total = gb[my_rows, :].astype(F32)
        for i in range(PLANE - 1):
            total += ra[i].astype(F32)
        rb[0] = total.astype(BF)
        for k in range(1, NZ):
            b_copy(k).start()
        for k in range(1, NZ):
            b_copy(k).wait_recv()
        full = rb[0].astype(F32)
        for k in range(1, NZ):
            full += rb[k].astype(F32)
        fin[my_rows, :] = (full * scale).astype(BF)

        @pl.loop(1, PLANE)
        def _(k):
            c_copy(k).start()

    for j in range(NCHUNK):
        @pl.when(place != OWNERS[j])
        def _(j=j):
            rows = fin.at[pl.ds(CHUNK * j, CHUNK)]
            pltpu.make_async_copy(rows, rows, c_recv.at[j]).wait()

    gr_ref[...] = fin[...]

    for i in range(10):
        h_sent(i)
    for i in range(8):
        g_sent(i)
    for j in range(NCHUNK):
        pl.when(place != OWNERS[j])(lambda j=j: a_copy(j).wait_send())

    @pl.when(is_owner)
    def _():
        for k in range(1, NZ):
            b_copy(k).wait_send()

        @pl.loop(1, PLANE)
        def _(k):
            c_copy(k).wait_send()


def shards(field, cotangent, first_filter, second_filter):
    scale = 1.0 / math.sqrt(TR * LONG * TC * SHORT)
    any_spec = pl.BlockSpec(memory_space=pl.ANY)
    vmem = pl.BlockSpec(memory_space=pltpu.VMEM)
    dma = pltpu.SemaphoreType.DMA

    def buf(*shape, dtype=BF):
        return pltpu.VMEM(shape, dtype)

    gf, gr = pl.pallas_call(
        lambda *refs: kernel(scale, *refs),
        out_shape=(jax.ShapeDtypeStruct((TR, CH, TC), BF), jax.ShapeDtypeStruct((K, 2 * CH), BF)),
        in_specs=[any_spec, any_spec, vmem, vmem],
        out_specs=(vmem, vmem),
        scratch_shapes=[
            buf(CH, TR, TC), buf(CH, TR, TC), buf(TR, CH, TC), buf(TR, CH, TC),
            buf(3, TR + 8, CH, TC), buf(3, TR + 16, CH, TC), buf(3, TR + 8, CH, TC),
            buf(2, 2, CH, 128), buf(4, CH, 128), buf(4, CH, 128),
            buf(2, CH, 128), buf(3, CH, 128), buf(3, CH, 128),
            buf(CH, K), buf(CH, K), buf(CH, K),
            buf(K, CH, dtype=F32), buf(CH, K, dtype=F32), buf(K, 2 * CH),
            buf(PLANE - 1, CHUNK, 2 * CH), buf(NZ, CHUNK, 2 * CH), buf(K, 2 * CH),
            dma((2,)), dma((10,)), dma((10,)), dma((8,)), dma((8,)),
            dma((NCHUNK,)), dma, dma((NZ - 1,)), dma((NZ - 1,)), dma((PLANE - 1,)), dma((NCHUNK,)),
        ],
        compiler_params=pltpu.CompilerParams(
            collective_id=0, has_side_effects=True, vmem_limit_bytes=40 << 20),
        name="dilated_backward",
    )(field, cotangent, first_filter, second_filter)
    grads = gr.astype(F32).reshape(9, CH, 2 * CH)
    return gf.transpose(1, 0, 2), grads[:, :, CH:], grads[:, :, :CH]


def solution(mesh):
    in_specs = (P(None, "long", "short"), P(None, "long", "short"), P(), P())
    out_specs = (P(None, "long", "short"), P(), P())
    return jax.shard_map(shards, mesh=mesh, in_specs=in_specs, out_specs=out_specs, check_vma=False)
```

time: 418 us -> 57 us (0.14)
  waiting for transfers between devices: 287 us -> 0 us
  Pallas kernels: 0 us -> 50.3 us
  starting transfers between devices: 47.3 us -> 0 us
  local copies, waits for them, and re-layouts: 36.2 us -> 5.83 us
  other arithmetic: 17.2 us -> 0 us
  between operations: 14.8 us -> 0.65 us
  matrix products: 14 us -> 0 us
    psum x1 -> x0, waiting for transfers between devices: 278 us -> none  [shards(): lax.psum((local_first, local_second), ('long', 'short'))]
    pallas_call x0 -> x1, Pallas kernels: none -> 50.3 us  [shards(): pl.pallas_call(lambda *refs: kernel(scale, *refs), out_shape=(jax.ShapeDt...]
    ppermute x16 -> x0, starting transfers between devices: 47.3 us -> none  [the longest x8 33.5 us: with_halo(): lax.ppermute(lax.slice_in_dim(block, block.shape[dim] - width, None, axis...]
    unnamed x49 -> x9, local copies, waits for them, and re-layouts: 16.4 us -> 4.98 us
    ppermute x16 -> x0, waiting for transfers between devices: 9.14 us -> none  [the longest x8 5.86 us: with_halo(): lax.ppermute(lax.slice_in_dim(block, 0, width, axis=dim), axis, backward)]
    concatenate x5 -> x0, other arithmetic: 8.86 us -> none  [with_halo(): block = jnp.concatenate([low, block, high], axis=dim)]
    dot_general x18 -> x0, matrix products: 7.34 us -> none  [correlate(): jnp.einsum('orc,irc->oi', grad, window, preferred_element_type=jnp.float32)]
    conv_general_dilated x12 -> x0, local copies, waits for them, and re-layouts: 7.05 us -> none  [dilated(): lax.conv_general_dilated(padded[None], kernel, (1, 1), 'VALID', rhs_dilat...]
  transfers between devices with their start and end apart: 17 -> 0, of which waited for: 5 -> 0; matrix products, arithmetic and copies ran while one was open for 13% -> 0% of each run, Pallas kernels for 0% -> 0%
where the time goes in v1:
time: 57 us; the launch traced here: 56.8 us
  Pallas kernels  50.3 us (88%)
  local copies, waits for them, and re-layouts  5.83 us (10%)
  between operations  0.65 us (1%)
    pallas_call x1, Pallas kernels, shards(): pl.pallas_call(lambda *refs: kernel(scale, *refs), out_shape=(jax.ShapeDt...  50.3 us
    unnamed x9, local copies, waits for them, and re-layouts  4.98 us

profile of v1, /device:TPU:1, one launch (start us, length us, event | category | flops | bytes accessed | tf_op | source)
XLA Modules:
  0.0 56.8 jit_solution(8798317128455184903)
XLA Ops:
  0.6 0.0 copy-start
  0.6 1.0 %copy-done = bf16[64,16,256]{2,1,0:T(8,128)(2,1)S(1)} copy-done((bf16[64,16,256]{2,1,0:T(8,128)(2,1)S(1)}, bf16[64,16,256]{2,1,0:T(8,128)(2,1)}, u32[]{:S(2)}) %copy-start) | copy-done | bytes 524312
  1.7 0.0 copy-start.1
  1.7 1.0 %copy-done.1 = bf16[64,16,256]{2,1,0:T(8,128)(2,1)S(1)} copy-done((bf16[64,16,256]{2,1,0:T(8,128)(2,1)S(1)}, bf16[64,16,256]{2,1,0:T(8,128)(2,1)}, u32[]{:S(2)}) %copy-start.1) | copy-done | bytes 524312
  2.7 0.0 copy-start.2
  2.7 0.9 %copy-done.2 = bf16[9,64,64]{2,1,0:T(8,128)(2,1)S(1)} copy-done((bf16[9,64,64]{2,1,0:T(8,128)(2,1)S(1)}, bf16[9,64,64]{2,1,0:T(8,128)(2,1)}, u32[]{:S(2)}) %copy-start.2) | copy-done | bytes 73752
  3.6 0.0 copy-start.3
  3.6 0.9 %copy-done.3 = bf16[9,64,64]{2,1,0:T(8,128)(2,1)S(1)} copy-done((bf16[9,64,64]{2,1,0:T(8,128)(2,1)S(1)}, bf16[9,64,64]{2,1,0:T(8,128)(2,1)}, u32[]{:S(2)}) %copy-start.3) | copy-done | bytes 73752
  4.5 50.3 %dilated_backward.1 = (bf16[16,64,256]{2,1,0:T(8,128)(2,1)S(1)}, bf16[576,128]{1,0:T(8,128)(2,1)S(1)}) custom-call(bf16[64,16,256]{2,1,0:T(8,128)(2,1)S(1)} %copy-done, bf16[64,16,256]{2,1,0:T(8,128)(2,1)S(1)} %copy-done.1, bf16[9,64,64]{2,1,0:T(8,128)(2,1)S(1)} %copy-done.2, bf16[9,64,64]{2,1,0:T(8,128)(2,1)S(1)} %copy-done.3), custom_call_target="tpu_custom_call" | custom-call | tf_op jit(solution)/shard_map/dilated_backward/pallas_call | solution.py:341
  54.9 1.1 %copy.7 = bf16[64,16,256]{2,1,0:T(8,128)(2,1)} copy(bf16[64,16,256]{2,0,1:T(8,128)(2,1)S(1)} %bitcast.4) | data formatting | bytes 1048576
  56.0 0.9 %fusion = (f32[9,64,64]{2,1,0:T(8,128)}, f32[9,64,64]{2,1,0:T(8,128)}) fusion(bf16[9,64,128]{2,1,0:T(8,128)(2,1)S(1)} %bitcast.3), kind=kLoop, calls=%fused_computation | loop fusion | bytes 589824 | tf_op jit(solution)/shard_map/slice | solution.py:362
Async XLA Ops:
  0.6 1.0 %copy-start = (bf16[64,16,256]{2,1,0:T(8,128)(2,1)S(1)}, bf16[64,16,256]{2,1,0:T(8,128)(2,1)}, u32[]{:S(2)}) copy-start(bf16[64,16,256]{2,1,0:T(8,128)(2,1)} %refs_0_.1) | copy-start | bytes 1572868
  1.7 1.0 %copy-start.1 = (bf16[64,16,256]{2,1,0:T(8,128)(2,1)S(1)}, bf16[64,16,256]{2,1,0:T(8,128)(2,1)}, u32[]{:S(2)}) copy-start(bf16[64,16,256]{2,1,0:T(8,128)(2,1)} %refs_1_.1) | copy-start | bytes 1572868
  2.7 0.9 %copy-start.2 = (bf16[9,64,64]{2,1,0:T(8,128)(2,1)S(1)}, bf16[9,64,64]{2,1,0:T(8,128)(2,1)}, u32[]{:S(2)}) copy-start(bf16[9,64,64]{2,1,0:T(8,128)(2,1)} %refs_2_.1) | copy-start | bytes 221188
  3.6 0.9 %copy-start.3 = (bf16[9,64,64]{2,1,0:T(8,128)(2,1)S(1)}, bf16[9,64,64]{2,1,0:T(8,128)(2,1)}, u32[]{:S(2)}) copy-start(bf16[9,64,64]{2,1,0:T(8,128)(2,1)} %refs_3_.1) | copy-start | bytes 221188

commit v2 on v1

v2 whole, which is shorter than its diff:
```python
import math

import jax
import jax.numpy as jnp
from jax import lax
from jax.experimental import pallas as pl
from jax.experimental.pallas import tpu as pltpu
from jax.sharding import PartitionSpec as P

BF = jnp.bfloat16
F32 = jnp.float32
MESH = pl.DeviceIdType.MESH
CH, TR, TC = 64, 16, 256
K = 9 * CH
LONG, SHORT = 64, 4
PLANE = 32
NZ = LONG // PLANE * SHORT
CHUNK = 32
NCHUNK = K // CHUNK
OWNERS = (1,) + tuple(range(2, 32, 2)) + (11, 21)

NEAR = ((-1, 0), (1, 0), (0, -1), (0, 1), (-1, -1), (-1, 1), (1, -1), (1, 1))


def ring_distance(a, n):
    return min(a % n, -a % n)


PLANE_STEPS = sorted(
    [(y, x, c) for y in range(4) for x in range(4) for c in range(2) if (y, x, c) != (0, 0, 0)],
    key=lambda t: -(ring_distance(t[0], 4) + ring_distance(t[1], 4)))
Z_STEPS = sorted(range(1, NZ), key=lambda k: -ring_distance(k, NZ))


def nt_dot(a, b):
    return lax.dot_general(a, b, (((1,), (1,)), ((), ())), preferred_element_type=F32)


def dot(a, b):
    return jnp.dot(a, b, preferred_element_type=F32)


def arrived(ref, sem):
    pltpu.make_async_copy(ref, ref, sem).wait()


def kernel(scale, field_hbm, cot_hbm, w1_hbm, w2_hbm, gf_ref, gr_ref,
           raw_f, raw_c, raw_w1, raw_w2, xf, a2, fs, cs, gs, ps, pleft, pright, gps, gleft, gright,
           w1c, w1t, w2own, w2halo, up_own, acc2, acc1, gb, ra, rb, fin, in_sem,
           f_send, f_recv, c_send, c_recv, p_send, p_recv, g_send, g_recv,
           a_send, a_recv, b_send, b_recv, o_send, o_recv):
    l = lax.axis_index("long")
    s = lax.axis_index("short")
    place = lax.rem(l, PLANE)
    base = l - place
    core = lax.rem(l, 2)
    z = lax.div(l, PLANE) * SHORT + s

    fetch = [pltpu.make_async_copy(src, dst, in_sem.at[i]) for i, (src, dst) in enumerate(
        ((field_hbm, raw_f), (cot_hbm, raw_c), (w1_hbm, raw_w1), (w2_hbm, raw_w2)))]
    for copy in fetch:
        copy.start()

    barrier = pltpu.get_barrier_semaphore()

    def greet(dev):
        pl.semaphore_signal(barrier, inc=1, device_id=dev, device_id_type=MESH)

    def there(dl, ds):
        ok = None
        for d, at, n in ((dl, l, LONG), (ds, s, SHORT)):
            if d == 0:
                continue
            here = at + d >= 0 if d < 0 else at + d < n
            ok = here if ok is None else jnp.logical_and(ok, here)
        return ok

    def plane_peer(step):
        y, x, c = step
        py = lax.rem(lax.div(place, 8) + y, 4)
        px = lax.rem(lax.div(place, 2) + x, 4)
        return base + py * 8 + px * 2 + lax.rem(core + c, 2), s

    def z_peer(k):
        other = lax.rem(z + k, NZ)
        return lax.div(other, SHORT) * PLANE + place, lax.rem(other, SHORT)

    greetings = jnp.int32(PLANE - 1 + NZ - 1)
    for dl, ds in NEAR:
        pl.when(there(dl, ds))(lambda dl=dl, ds=ds: greet((l + dl, s + ds)))
        greetings = greetings + there(dl, ds).astype(jnp.int32)
    for k in Z_STEPS:
        greet(z_peer(k))
    for step in PLANE_STEPS:
        greet(plane_peer(step))

    def message(dl, ds, src, dst, send_sem, recv_sem):
        copy = pltpu.make_async_remote_copy(
            src_ref=src, dst_ref=dst, send_sem=send_sem, recv_sem=recv_sem,
            device_id=(l + dl, s + ds), device_id_type=MESH)
        ok = there(dl, ds)
        return (lambda: pl.when(ok)(lambda: copy.start()),
                lambda: pl.when(ok)(lambda: copy.wait_send()))

    def receive(ok, dst, sem):
        pl.when(ok)(lambda: arrived(dst, sem))

        @pl.when(jnp.logical_not(ok))
        def _():
            dst[...] = jnp.zeros(dst.shape, dst.dtype)

    f_out = [message(-1, 0, fs.at[1, pl.ds(4, 4)], fs.at[1, pl.ds(20, 4)], f_send.at[0], f_recv.at[1]),
             message(1, 0, fs.at[1, pl.ds(16, 4)], fs.at[1, pl.ds(0, 4)], f_send.at[1], f_recv.at[0])]
    c_out = [message(-1, 0, cs.at[1, pl.ds(8, 8)], cs.at[1, pl.ds(24, 8)], c_send.at[0], c_recv.at[1]),
             message(1, 0, cs.at[1, pl.ds(16, 8)], cs.at[1, pl.ds(0, 8)], c_send.at[1], c_recv.at[0])]
    g_out = [message(-1, 0, gs.at[1, pl.ds(4, 4)], gs.at[1, pl.ds(20, 4)], g_send.at[0], g_recv.at[7]),
             message(1, 0, gs.at[1, pl.ds(16, 4)], gs.at[1, pl.ds(0, 4)], g_send.at[1], g_recv.at[6])]
    p_out = []
    for side, (ds, into, g_into) in enumerate(((-1, pright, gright), (1, pleft, gleft))):
        p_out.append(message(0, ds, ps.at[side], into.at[pl.ds(1, 2)], p_send.at[side], p_recv.at[1 - side]))
        g_out.append(message(0, ds, gps.at[side], g_into.at[1], g_send.at[2 + side], g_recv.at[1 - side]))
    for half, dl in ((0, -1), (1, 1)):
        for side, (ds, into, g_into) in enumerate(((-1, pright, gright), (1, pleft, gleft))):
            out, back = 2 + 2 * half + side, 2 + 2 * (1 - half) + 1 - side
            p_out.append(message(
                dl, ds, ps.at[side, pl.ds(half, 1)], into.at[pl.ds(3 - 3 * half, 1)], p_send.at[out], p_recv.at[back]))
            g_out.append(message(
                dl, ds, gps.at[side], g_into.at[2 - 2 * half], g_send.at[2 + out], g_recv.at[back]))

    fetch[0].wait()
    own_f = jnp.swapaxes(raw_f[...], 0, 1)
    xf[...] = own_f
    fs[1, 4:20] = jnp.maximum(own_f, 0)
    fetch[1].wait()
    cs[1, 8:24] = jnp.swapaxes(raw_c[...], 0, 1)
    for half in range(2):
        for side in range(2):
            c8 = 0 if side == 0 else TC - 8
            c4 = 0 if side == 0 else TC - 4
            pieces = [cs[1, 8 + 8 * half + k][:, c8:c8 + 8] for k in range(8)]
            pieces += [fs[1, 4 + 8 * half + k][:, c4:c4 + 4] for k in range(8)]
            pieces += [jnp.zeros((CH, 32), BF)]
            ps[side, half] = jnp.concatenate(pieces, axis=1)

    pl.semaphore_wait(barrier, greetings)
    for start, _ in f_out + p_out + c_out:
        start()

    fetch[2].wait()
    fetch[3].wait()
    for t in range(9):
        w1c[:, CH * t:CH * (t + 1)] = raw_w1[t]
    w1t[...] = raw_w1[...].reshape(K, CH).T
    taps_of = [raw_w2[3 * a:3 * a + 3].reshape(3 * CH, CH).T for a in range(3)]
    for half in range(2):
        w2own[half] = jnp.concatenate([taps_of[1], taps_of[2 * half]], axis=1)
        w2halo[half] = taps_of[2 - 2 * half]

    acc2[...] = jnp.zeros_like(acc2)
    acc1[...] = jnp.zeros_like(acc1)

    def shift_left(x, h, at, d):
        return jnp.concatenate([x[:, d:], h[:, at:at + d]], axis=1)

    def shift_right(x, h, at, d):
        return jnp.concatenate([h[:, at:at + d], x[:, :TC - d]], axis=1)

    def f_row(blk, k, e):
        x = fs[1, e]
        fs[0, e] = shift_right(x, pleft[blk], 64 + 4 * k, 4)
        fs[2, e] = shift_left(x, pright[blk], 64 + 4 * k, 4)

    def c_row(blk, k):
        e = 8 * blk + k
        x = cs[1, e]
        cs[2, e] = shift_right(x, pleft[blk], 8 * k, 8)
        cs[0, e] = shift_left(x, pright[blk], 8 * k, 8)

    def taps(ref, rows):
        return [ref[b, e] for e in rows for b in range(3)]

    def stack(parts):
        return jnp.concatenate(parts, axis=0)

    receive(there(0, -1), pleft.at[pl.ds(1, 2)], p_recv.at[0])
    receive(there(0, 1), pright.at[pl.ds(1, 2)], p_recv.at[1])

    @pl.loop(1, 3)
    def _(blk):
        for k in range(8):
            f_row(blk, k, 8 * blk + k - 4)
            c_row(blk, k)

    def hidden_row(r):
        h = xf[r].astype(F32) + dot(w1c[...], stack(taps(fs, [r, r + 4, r + 8])))
        a2[r] = jnp.maximum(h.astype(BF), 0)

    @pl.loop(1, 3)
    def _(g):
        for k in range(4):
            hidden_row(4 * g + k)

    for half in range(2):
        @pl.loop(0, 2)
        def _(g):
            for k in range(4):
                r = 8 * half + 4 * g + k
                up_own[r] = dot(w2own[half], stack(taps(cs, [r + 8, r + 16 - 16 * half])))

    @pl.loop(0, 2)
    def _(i):
        half = (1 - core) + i * (2 * core - 1)
        ok = jnp.logical_or(jnp.logical_and(half == 0, l > 0), jnp.logical_and(half == 1, l < LONG - 1))
        receive(jnp.logical_and(ok, s > 0), pleft.at[pl.ds(3 * half, 1)], p_recv.at[2 + 2 * half])
        receive(jnp.logical_and(ok, s < SHORT - 1), pright.at[pl.ds(3 * half, 1)], p_recv.at[3 + 2 * half])
        receive(ok, fs.at[1, pl.ds(20 * half, 4)], f_recv.at[half])
        for k in range(4):
            e = 20 * half + k
            x = fs[1, e]
            for b, shift, pack in ((0, shift_right, pleft), (2, shift_left, pright)):
                low = shift(x, pack[3 * half], 64 + 4 * k, 4)
                high = shift(x, pack[3 * half], 64 + 4 * (k + 4), 4)
                fs[b, e] = jnp.where(half == 1, low, high)
        for k in range(4):
            hidden_row(12 * half + k)

        rows = [8 * half + k for k in range(8)]
        act = jnp.concatenate([a2[r] for r in rows], axis=1)
        own = nt_dot(
            jnp.concatenate([stack(taps(cs, [r + 8, r + 16 - 16 * half])) for r in rows], axis=1), act)
        acc2[1] += own[:3 * CH]
        acc2[2 * half] += own[3 * CH:]

        receive(ok, cs.at[1, pl.ds(24 * half, 8)], c_recv.at[half])
        for k in range(8):
            c_row(3 * half, k)
        beyond = [stack(taps(cs, [24 * half + k])) for k in range(8)]
        for k, r in enumerate(rows):
            up = up_own[r] + dot(w2halo[half], beyond[k])
            gh = cs[1, r + 8].astype(F32) + jnp.where(a2[r].astype(F32) > 0, up, 0.0)
            gs[1, r + 4] = gh.astype(BF)
        acc2[2 - 2 * half] += nt_dot(jnp.concatenate(beyond, axis=1), act)
        acc1[...] += nt_dot(
            jnp.concatenate([gs[1, r + 4] for r in rows], axis=1),
            jnp.concatenate([stack(taps(fs, [r, r + 4, r + 8])) for r in rows], axis=1))

    for t in range(9):
        gb[CH * t:CH * (t + 1), :] = jnp.concatenate(
            [acc2[t // 3, CH * (t % 3):CH * (t % 3 + 1), :], acc1[:, CH * t:CH * (t + 1)]], axis=1).astype(BF)

    def a_copy(j):
        owner = OWNERS[j]
        slot = lax.rem(place - owner + PLANE - 1, PLANE)
        return pltpu.make_async_remote_copy(
            src_ref=gb.at[pl.ds(CHUNK * j, CHUNK)], dst_ref=ra.at[slot],
            send_sem=a_send.at[j], recv_sem=a_recv,
            device_id=(base + owner, s), device_id_type=MESH)

    for j in range(NCHUNK):
        pl.when(place != OWNERS[j])(lambda j=j: a_copy(j).start())

    for start, _ in g_out[:2]:
        start()
    for side in range(2):
        c4 = 0 if side == 0 else TC - 4
        pieces = [gs[1, 4 + k][:, c4:c4 + 4] for k in range(16)] + [jnp.zeros((CH, 64), BF)]
        gps[side] = jnp.concatenate(pieces, axis=1)
    for start, _ in g_out[2:]:
        start()

    is_owner = jnp.logical_or(
        jnp.logical_and(core == 0, place > 0),
        jnp.logical_or(place == 1, jnp.logical_or(place == 11, place == 21)))
    mine = jnp.where(place == 11, 16, jnp.where(place == 21, 17, lax.div(place, 2)))
    my_rows = pl.ds(pl.multiple_of(CHUNK * mine, CHUNK), CHUNK)

    def b_copy(k):
        return pltpu.make_async_remote_copy(
            src_ref=rb.at[0], dst_ref=rb.at[k], send_sem=b_send.at[k - 1], recv_sem=b_recv.at[k - 1],
            device_id=z_peer(k), device_id_type=MESH)

    def o_copy(n):
        return pltpu.make_async_remote_copy(
            src_ref=fin.at[my_rows], dst_ref=fin.at[my_rows], send_sem=o_send.at[n],
            recv_sem=o_recv.at[mine], device_id=plane_peer(PLANE_STEPS[n]), device_id_type=MESH)

    @pl.when(is_owner)
    def _():
        arrived(ra, a_recv)
        total = gb[my_rows, :].astype(F32)
        for i in range(PLANE - 1):
            total += ra[i].astype(F32)
        rb[0] = total.astype(BF)
        for k in Z_STEPS:
            b_copy(k).start()

    receive(there(-1, 0), gs.at[1, pl.ds(0, 4)], g_recv.at[6])
    receive(there(1, 0), gs.at[1, pl.ds(20, 4)], g_recv.at[7])
    for side, (ds, into) in enumerate(((-1, gleft), (1, gright))):
        receive(there(0, ds), into.at[1], g_recv.at[side])
        receive(there(-1, ds), into.at[0], g_recv.at[2 + side])
        receive(there(1, ds), into.at[2], g_recv.at[4 + side])

    def g_row(blk, e, at):
        x = gs[1, e]
        gs[2, e] = shift_right(x, gleft[blk], at, 4)
        gs[0, e] = shift_left(x, gright[blk], at, 4)

    for k in range(16):
        g_row(1, 4 + k, 4 * k)
    for k in range(4):
        g_row(0, k, 4 * (12 + k))
        g_row(2, 20 + k, 4 * k)

    @pl.loop(0, TR // 4)
    def _(g):
        for k in range(4):
            r = 4 * g + k
            back = dot(w1t[...], stack(taps(gs, [r + 8, r + 4, r])))
            out = gs[1, r + 4].astype(F32) + jnp.where(xf[r].astype(F32) > 0, back, 0.0)
            gf_ref[r] = out.astype(BF)

    @pl.when(is_owner)
    def _():
        full = rb[0].astype(F32)
        for k in reversed(Z_STEPS):
            b_copy(k).wait_recv()
            full += rb[k].astype(F32)
        fin[my_rows, :] = (full * scale).astype(BF)
        for n in range(PLANE - 1):
            o_copy(n).start()

    for _, sent in f_out + p_out + c_out + g_out:
        sent()
    for j in range(NCHUNK):
        pl.when(place != OWNERS[j])(lambda j=j: a_copy(j).wait_send())

    for j in range(NCHUNK):
        pl.when(place != OWNERS[j])(
            lambda j=j: arrived(fin.at[pl.ds(CHUNK * j, CHUNK)], o_recv.at[j]))
    gr_ref[...] = fin[...]

    @pl.when(is_owner)
    def _():
        for k in Z_STEPS:
            b_copy(k).wait_send()
        for n in range(PLANE - 1):
            o_copy(n).wait_send()


def shards(field, cotangent, first_filter, second_filter):
    scale = 1.0 / math.sqrt(TR * LONG * TC * SHORT)
    hbm = pl.BlockSpec(memory_space=pltpu.HBM)
    vmem = pl.BlockSpec(memory_space=pltpu.VMEM)
    dma = pltpu.SemaphoreType.DMA

    def buf(*shape, dtype=BF):
        return pltpu.VMEM(shape, dtype)

    gf, gr = pl.pallas_call(
        lambda *refs: kernel(scale, *refs),
        out_shape=(jax.ShapeDtypeStruct((TR, CH, TC), BF), jax.ShapeDtypeStruct((K, 2 * CH), BF)),
        in_specs=[hbm] * 4,
        out_specs=(vmem, vmem),
        scratch_shapes=[
            buf(CH, TR, TC), buf(CH, TR, TC), buf(9, CH, CH), buf(9, CH, CH),
            buf(TR, CH, TC), buf(TR, CH, TC),
            buf(3, TR + 8, CH, TC), buf(3, TR + 16, CH, TC), buf(3, TR + 8, CH, TC),
            buf(2, 2, CH, 128), buf(4, CH, 128), buf(4, CH, 128),
            buf(2, CH, 128), buf(3, CH, 128), buf(3, CH, 128),
            buf(CH, K), buf(CH, K), buf(2, CH, 6 * CH), buf(2, CH, 3 * CH),
            buf(TR, CH, TC, dtype=F32),
            buf(3, 3 * CH, CH, dtype=F32), buf(CH, K, dtype=F32), buf(K, 2 * CH),
            buf(PLANE - 1, CHUNK, 2 * CH), buf(NZ, CHUNK, 2 * CH), buf(K, 2 * CH),
            dma((4,)),
            dma((2,)), dma((2,)), dma((2,)), dma((2,)), dma((6,)), dma((6,)), dma((8,)), dma((8,)),
            dma((NCHUNK,)), dma, dma((NZ - 1,)), dma((NZ - 1,)), dma((PLANE - 1,)), dma((NCHUNK,)),
        ],
        compiler_params=pltpu.CompilerParams(
            collective_id=0, has_side_effects=True, vmem_limit_bytes=60 << 20),
        name="dilated_backward",
    )(field, cotangent, first_filter, second_filter)
    grads = gr.astype(F32).reshape(9, CH, 2 * CH)
    return gf.transpose(1, 0, 2), grads[:, :, CH:], grads[:, :, :CH]


def solution(mesh):
    in_specs = (P(None, "long", "short"), P(None, "long", "short"), P(), P())
    out_specs = (P(None, "long", "short"), P(), P())
    return jax.shard_map(shards, mesh=mesh, in_specs=in_specs, out_specs=out_specs, check_vma=False)
```

time: 57 us -> 48.8 us (0.86)
  Pallas kernels: 50.3 us -> 45 us
  local copies, waits for them, and re-layouts: 5.83 us -> 3.02 us
    pallas_call x1, Pallas kernels: 50.3 us -> 45 us  [shards(): pl.pallas_call(lambda *refs: kernel(scale, *refs), out_shape=(jax.ShapeDt...]
    unnamed x9 -> x3, local copies, waits for them, and re-layouts: 4.98 us -> 2.17 us
where the time goes in v2:
time: 48.8 us; the launch traced here: 48.7 us
  Pallas kernels  45 us (92%)
  local copies, waits for them, and re-layouts  3.02 us (6%)
  between operations  0.65 us (1%)
    pallas_call x1, Pallas kernels, shards(): pl.pallas_call(lambda *refs: kernel(scale, *refs), out_shape=(jax.ShapeDt...  45 us
    unnamed x3, local copies, waits for them, and re-layouts  2.17 us

profile of v2, /device:TPU:1, one launch (start us, length us, event | category | flops | bytes accessed | tf_op | source)
XLA Modules:
  0.0 48.7 jit_solution(1600377623972766434)
XLA Ops:
  0.6 45.0 %dilated_backward.1 = (bf16[16,64,256]{2,1,0:T(8,128)(2,1)}, bf16[576,128]{1,0:T(8,128)(2,1)}) custom-call(bf16[64,16,256]{2,1,0:T(8,128)(2,1)} %refs_0_.1, bf16[64,16,256]{2,1,0:T(8,128)(2,1)} %refs_1_.1, bf16[9,64,64]{2,1,0:T(8,128)(2,1)} %refs_2_.1, bf16[9,64,64]{2,1,0:T(8,128)(2,1)} %refs_3_.1), custom_call_target="tpu_custom_call" | custom-call | tf_op jit(solution)/shard_map/dilated_backward/pallas_call | solution.py:360
  45.7 0.0 copy-start
  45.7 2.2 %copy.7 = bf16[64,16,256]{2,1,0:T(8,128)(2,1)} copy(bf16[64,16,256]{2,0,1:T(8,128)(2,1)} %bitcast.4) | data formatting | bytes 1048576
  47.8 0.0 copy-done
  47.8 0.9 %fusion = (f32[9,64,64]{2,1,0:T(8,128)}, f32[9,64,64]{2,1,0:T(8,128)}) fusion(bf16[9,64,128]{2,1,0:T(8,128)(2,1)S(1)} %bitcast.3), kind=kLoop, calls=%fused_computation | loop fusion | bytes 589824 | tf_op jit(solution)/shard_map/slice | solution.py:384
Async XLA Ops:
  45.7 2.2 %copy-start = (bf16[576,128]{1,0:T(8,128)(2,1)S(1)}, bf16[576,128]{1,0:T(8,128)(2,1)}, u32[]{:S(2)}) copy-start(bf16[576,128]{1,0:T(8,128)(2,1)} %get-tuple-element.6) | copy-start | bytes 442372

commit v3 on v2

--- a/solution.py
+++ b/solution.py
@@ -17,7 +17,7 @@
 NZ = LONG // PLANE * SHORT
 CHUNK = 32
 NCHUNK = K // CHUNK
-OWNERS = (1,) + tuple(range(2, 32, 2)) + (11, 21)
+OWNERS = (8, 9, 22, 23, 2, 28, 16, 17, 4, 5, 14, 15, 26, 27, 24, 25, 6, 7)
 
 NEAR = ((-1, 0), (1, 0), (0, -1), (0, 1), (-1, -1), (-1, 1), (1, -1), (1, 1))
 
@@ -48,7 +48,7 @@
            raw_f, raw_c, raw_w1, raw_w2, xf, a2, fs, cs, gs, ps, pleft, pright, gps, gleft, gright,
            w1c, w1t, w2own, w2halo, up_own, acc2, acc1, gb, ra, rb, fin, in_sem,
            f_send, f_recv, c_send, c_recv, p_send, p_recv, g_send, g_recv,
-           a_send, a_recv, b_send, b_recv, o_send, o_recv):
+           a_send, a_recv, b_send, b_recv, o_send, o_recv, ready, out_sem):
     l = lax.axis_index("long")
     s = lax.axis_index("short")
     place = lax.rem(l, PLANE)
@@ -85,14 +85,19 @@
         other = lax.rem(z + k, NZ)
         return lax.div(other, SHORT) * PLANE + place, lax.rem(other, SHORT)
 
-    greetings = jnp.int32(PLANE - 1 + NZ - 1)
+    row_steps = [step for step in PLANE_STEPS if step[0] == 0]
+    column_steps = [step for step in PLANE_STEPS if step[1:] == (0, 0)]
+    first = [plane_peer(step) for step in row_steps + column_steps] + [z_peer(1), z_peer(NZ - 1)]
+    greetings = jnp.int32(len(first))
     for dl, ds in NEAR:
         pl.when(there(dl, ds))(lambda dl=dl, ds=ds: greet((l + dl, s + ds)))
         greetings = greetings + there(dl, ds).astype(jnp.int32)
-    for k in Z_STEPS:
-        greet(z_peer(k))
-    for step in PLANE_STEPS:
-        greet(plane_peer(step))
+    for dev in first:
+        greet(dev)
+
+    def pass_on(n, devs):
+        for dev in devs:
+            pl.semaphore_signal(ready.at[n], inc=1, device_id=dev, device_id_type=MESH)
 
     def message(dl, ds, src, dst, send_sem, recv_sem):
         copy = pltpu.make_async_remote_copy(
@@ -145,6 +150,8 @@
     pl.semaphore_wait(barrier, greetings)
     for start, _ in f_out + p_out + c_out:
         start()
+    pass_on(0, [plane_peer(step) for step in row_steps])
+    pass_on(1, [z_peer(1), z_peer(NZ - 1)])
 
     fetch[2].wait()
     fetch[3].wait()
@@ -184,6 +191,9 @@
 
     receive(there(0, -1), pleft.at[pl.ds(1, 2)], p_recv.at[0])
     receive(there(0, 1), pright.at[pl.ds(1, 2)], p_recv.at[1])
+    pl.semaphore_wait(ready.at[0], len(row_steps))
+    pl.semaphore_wait(ready.at[1], 2)
+    pass_on(2, [z_peer(2), z_peer(NZ - 2)])
 
     @pl.loop(1, 3)
     def _(blk):
@@ -258,6 +268,7 @@
 
     for j in range(NCHUNK):
         pl.when(place != OWNERS[j])(lambda j=j: a_copy(j).start())
+    pl.semaphore_wait(ready.at[2], 2)
 
     for start, _ in g_out[:2]:
         start()
@@ -268,10 +279,11 @@
     for start, _ in g_out[2:]:
         start()
 
-    is_owner = jnp.logical_or(
-        jnp.logical_and(core == 0, place > 0),
-        jnp.logical_or(place == 1, jnp.logical_or(place == 11, place == 21)))
-    mine = jnp.where(place == 11, 16, jnp.where(place == 21, 17, lax.div(place, 2)))
+    mine = jnp.int32(0)
+    is_owner = place < 0
+    for j, owner in enumerate(OWNERS):
+        mine = jnp.where(place == owner, j, mine)
+        is_owner = jnp.logical_or(is_owner, place == owner)
     my_rows = pl.ds(pl.multiple_of(CHUNK * mine, CHUNK), CHUNK)
 
     def b_copy(k):
@@ -318,7 +330,11 @@
             r = 4 * g + k
             back = dot(w1t[...], stack(taps(gs, [r + 8, r + 4, r])))
             out = gs[1, r + 4].astype(F32) + jnp.where(xf[r].astype(F32) > 0, back, 0.0)
-            gf_ref[r] = out.astype(BF)
+            xf[r] = out.astype(BF)
+
+    raw_f[...] = jnp.swapaxes(xf[...], 0, 1)
+    write_gf = pltpu.make_async_copy(raw_f, gf_ref, out_sem.at[0])
+    write_gf.start()
 
     @pl.when(is_owner)
     def _():
@@ -338,7 +354,8 @@
     for j in range(NCHUNK):
         pl.when(place != OWNERS[j])(
             lambda j=j: arrived(fin.at[pl.ds(CHUNK * j, CHUNK)], o_recv.at[j]))
-    gr_ref[...] = fin[...]
+    write_gr = pltpu.make_async_copy(fin, gr_ref, out_sem.at[1])
+    write_gr.start()
 
     @pl.when(is_owner)
     def _():
@@ -347,6 +364,34 @@
         for n in range(PLANE - 1):
             o_copy(n).wait_send()
 
+    write_gf.wait()
+    write_gr.wait()
+
+
+def finish(gf_hbm, gr_hbm, out_hbm, first_hbm, second_hbm, gf, gr, first, second, load, store):
+    parts = 4
+    step = CH // parts
+    read = pltpu.make_async_copy(gr_hbm, gr, load.at[parts])
+    read.start()
+    blocks = [pl.ds(i * step, step) for i in range(parts)]
+    loads = [pltpu.make_async_copy(gf_hbm.at[b], gf.at[b], load.at[i]) for i, b in enumerate(blocks)]
+    stores = [pltpu.make_async_copy(gf.at[b], out_hbm.at[b], store.at[i]) for i, b in enumerate(blocks)]
+    for copy in loads:
+        copy.start()
+    read.wait()
+    both = gr[...].astype(F32).reshape(9, CH, 2 * CH)
+    first[...] = both[:, :, CH:]
+    second[...] = both[:, :, :CH]
+    stores.append(pltpu.make_async_copy(first, first_hbm, store.at[parts]))
+    stores.append(pltpu.make_async_copy(second, second_hbm, store.at[parts + 1]))
+    stores[parts].start()
+    stores[parts + 1].start()
+    for i in range(parts):
+        loads[i].wait()
+        stores[i].start()
+    for copy in stores:
+        copy.wait()
+
 
 def shards(field, cotangent, first_filter, second_filter):
     scale = 1.0 / math.sqrt(TR * LONG * TC * SHORT)
@@ -359,9 +404,9 @@
 
     gf, gr = pl.pallas_call(
         lambda *refs: kernel(scale, *refs),
-        out_shape=(jax.ShapeDtypeStruct((TR, CH, TC), BF), jax.ShapeDtypeStruct((K, 2 * CH), BF)),
+        out_shape=(jax.ShapeDtypeStruct((CH, TR, TC), BF), jax.ShapeDtypeStruct((K, 2 * CH), BF)),
         in_specs=[hbm] * 4,
-        out_specs=(vmem, vmem),
+        out_specs=(hbm, hbm),
         scratch_shapes=[
             buf(CH, TR, TC), buf(CH, TR, TC), buf(9, CH, CH), buf(9, CH, CH),
             buf(TR, CH, TC), buf(TR, CH, TC),
@@ -375,13 +420,23 @@
             dma((4,)),
             dma((2,)), dma((2,)), dma((2,)), dma((2,)), dma((6,)), dma((6,)), dma((8,)), dma((8,)),
             dma((NCHUNK,)), dma, dma((NZ - 1,)), dma((NZ - 1,)), dma((PLANE - 1,)), dma((NCHUNK,)),
+            pltpu.SemaphoreType.REGULAR((3,)), dma((2,)),
         ],
         compiler_params=pltpu.CompilerParams(
             collective_id=0, has_side_effects=True, vmem_limit_bytes=60 << 20),
         name="dilated_backward",
     )(field, cotangent, first_filter, second_filter)
-    grads = gr.astype(F32).reshape(9, CH, 2 * CH)
-    return gf.transpose(1, 0, 2), grads[:, :, CH:], grads[:, :, :CH]
+    taps = jax.ShapeDtypeStruct((9, CH, CH), F32)
+    return pl.pallas_call(
+        finish,
+        out_shape=(jax.ShapeDtypeStruct((CH, TR, TC), BF), taps, taps),
+        in_specs=[hbm, hbm],
+        out_specs=(hbm, hbm, hbm),
+        scratch_shapes=[
+            buf(CH, TR, TC), buf(K, 2 * CH), buf(9, CH, CH, dtype=F32), buf(9, CH, CH, dtype=F32), dma((5,)), dma((6,))],
+        compiler_params=pltpu.CompilerParams(vmem_limit_bytes=60 << 20),
+        name="finish",
+    )(gf, gr)
 
 
 def solution(mesh):

time: 48.8 us -> 46.3 us (0.949)
  local copies, waits for them, and re-layouts: 3.02 us -> 0 us
  Pallas kernels: 45 us -> 45.6 us
    unnamed x3 -> x0, local copies, waits for them, and re-layouts: 2.17 us -> none
    pallas_call x0 -> x1, Pallas kernels: none -> 2.1 us  [shards(): pl.pallas_call(finish, out_shape=(jax.ShapeDtypeStruct((CH, TR, TC), BF),...]
    pallas_call x1, Pallas kernels: 45 us -> 43.5 us  [shards(): pl.pallas_call(lambda *refs: kernel(scale, *refs), out_shape=(jax.ShapeDt...]
    slice x1 -> x0, local copies, waits for them, and re-layouts: 0.85 us -> none  [shards(): return (gf.transpose(1, 0, 2), grads[:, :, CH:], grads[:, :, :CH])]
where the time goes in v3:
time: 46.3 us; the launch traced here: 46.2 us
  Pallas kernels  45.6 us (98%)
  between operations  0.64 us (1%)
    pallas_call x1, Pallas kernels, shards(): pl.pallas_call(lambda *refs: kernel(scale, *refs), out_shape=(jax.ShapeDt...  43.5 us
    pallas_call x1, Pallas kernels, shards(): pl.pallas_call(finish, out_shape=(jax.ShapeDtypeStruct((CH, TR, TC), BF),...  2.1 us

profile of v3, /device:TPU:1, one launch (start us, length us, event | category | flops | bytes accessed | tf_op | source)
XLA Modules:
  0.0 46.2 jit_solution(3223295458827271490)
XLA Ops:
  0.6 43.5 %dilated_backward.1 = (bf16[64,16,256]{2,1,0:T(8,128)(2,1)}, bf16[576,128]{1,0:T(8,128)(2,1)}) custom-call(bf16[64,16,256]{2,1,0:T(8,128)(2,1)} %refs_0_.1, bf16[64,16,256]{2,1,0:T(8,128)(2,1)} %refs_1_.1, bf16[9,64,64]{2,1,0:T(8,128)(2,1)} %refs_2_.1, bf16[9,64,64]{2,1,0:T(8,128)(2,1)} %refs_3_.1), custom_call_target="tpu_custom_call" | custom-call | tf_op jit(solution)/shard_map/dilated_backward/pallas_call | solution.py:405
  44.1 2.1 %finish.1 = (bf16[64,16,256]{2,1,0:T(8,128)(2,1)}, f32[9,64,64]{2,1,0:T(8,128)}, f32[9,64,64]{2,1,0:T(8,128)}) custom-call(bf16[64,16,256]{2,1,0:T(8,128)(2,1)} %get-tuple-element.5.gf_hbm, bf16[576,128]{1,0:T(8,128)(2,1)} %get-tuple-element.6.gr_hbm), custom_call_target="tpu_custom_call" | custom-call | tf_op jit(solution)/shard_map/finish/pallas_call | solution.py:430

commit v4 on v3

--- a/solution.py
+++ b/solution.py
@@ -48,7 +48,8 @@
            raw_f, raw_c, raw_w1, raw_w2, xf, a2, fs, cs, gs, ps, pleft, pright, gps, gleft, gright,
            w1c, w1t, w2own, w2halo, up_own, acc2, acc1, gb, ra, rb, fin, in_sem,
            f_send, f_recv, c_send, c_recv, p_send, p_recv, g_send, g_recv,
-           a_send, a_recv, b_send, b_recv, o_send, o_recv, ready, out_sem):
+           a_send, a_recv, b_send, b_recv, o_send, o_recv, ready, out_sem,
+           relay, r_send, r_recv, w_send, w_recv):
     l = lax.axis_index("long")
     s = lax.axis_index("short")
     place = lax.rem(l, PLANE)
@@ -99,11 +100,11 @@
         for dev in devs:
             pl.semaphore_signal(ready.at[n], inc=1, device_id=dev, device_id_type=MESH)
 
-    def message(dl, ds, src, dst, send_sem, recv_sem):
+    def message(dl, ds, src, dst, send_sem, recv_sem, only=None):
         copy = pltpu.make_async_remote_copy(
             src_ref=src, dst_ref=dst, send_sem=send_sem, recv_sem=recv_sem,
             device_id=(l + dl, s + ds), device_id_type=MESH)
-        ok = there(dl, ds)
+        ok = there(dl, ds) if only is None else only
         return (lambda: pl.when(ok)(lambda: copy.start()),
                 lambda: pl.when(ok)(lambda: copy.wait_send()))
 
@@ -116,8 +117,23 @@
 
     f_out = [message(-1, 0, fs.at[1, pl.ds(4, 4)], fs.at[1, pl.ds(20, 4)], f_send.at[0], f_recv.at[1]),
              message(1, 0, fs.at[1, pl.ds(16, 4)], fs.at[1, pl.ds(0, 4)], f_send.at[1], f_recv.at[0])]
-    c_out = [message(-1, 0, cs.at[1, pl.ds(8, 8)], cs.at[1, pl.ds(24, 8)], c_send.at[0], c_recv.at[1]),
-             message(1, 0, cs.at[1, pl.ds(16, 8)], cs.at[1, pl.ds(0, 8)], c_send.at[1], c_recv.at[0])]
+    seam_down = jnp.logical_and(place == PLANE - 1, l < LONG - 1)
+    seam_up = jnp.logical_and(place == 0, l > 0)
+    up, down = jnp.logical_and(l > 0, place != 0), jnp.logical_and(l < LONG - 1, place != PLANE - 1)
+    c_out = [message(-1, 0, cs.at[1, pl.ds(8, 8)], cs.at[1, pl.ds(24, 8)], c_send.at[0], c_recv.at[1], up),
+             message(1, 0, cs.at[1, pl.ds(16, 8)], cs.at[1, pl.ds(0, 8)], c_send.at[1], c_recv.at[0], down),
+             message(-1, 0, cs.at[1, pl.ds(8, 4)], cs.at[1, pl.ds(24, 4)], c_send.at[0], c_recv.at[1], seam_up),
+             message(1, 0, cs.at[1, pl.ds(16, 4)], cs.at[1, pl.ds(0, 4)], c_send.at[1], c_recv.at[0], seam_down)]
+    relay_out, relay_on = [], []
+    for n, hop in enumerate((2, 8)):
+        for at_seam, way, low in ((seam_down, 1, 16), (seam_up, -1, 8)):
+            rows = pl.ds(low + 4 + 2 * n, 2)
+            relay_out.append(message(-way * hop, 0, cs.at[1, rows], relay, r_send.at[n], r_recv, at_seam))
+            end = PLANE - 1 - hop if way == 1 else hop
+            here = jnp.logical_and(place == end, l < PLANE if way == 1 else l >= LONG - PLANE)
+            into = pl.ds((0 if way == 1 else 24) + 4 + 2 * n, 2)
+            relay_on.append((here, message(
+                way * (hop + 1), 0, relay, cs.at[1, into], w_send, w_recv.at[n], here)))
     g_out = [message(-1, 0, gs.at[1, pl.ds(4, 4)], gs.at[1, pl.ds(20, 4)], g_send.at[0], g_recv.at[7]),
              message(1, 0, gs.at[1, pl.ds(16, 4)], gs.at[1, pl.ds(0, 4)], g_send.at[1], g_recv.at[6])]
     p_out = []
@@ -148,7 +164,7 @@
             ps[side, half] = jnp.concatenate(pieces, axis=1)
 
     pl.semaphore_wait(barrier, greetings)
-    for start, _ in f_out + p_out + c_out:
+    for start, _ in relay_out + f_out + p_out + c_out:
         start()
     pass_on(0, [plane_peer(step) for step in row_steps])
     pass_on(1, [z_peer(1), z_peer(NZ - 1)])
@@ -191,6 +207,9 @@
 
     receive(there(0, -1), pleft.at[pl.ds(1, 2)], p_recv.at[0])
     receive(there(0, 1), pright.at[pl.ds(1, 2)], p_recv.at[1])
+    for here, (start, _) in relay_on:
+        pl.when(here)(lambda: arrived(relay, r_recv))
+        start()
     pl.semaphore_wait(ready.at[0], len(row_steps))
     pl.semaphore_wait(ready.at[1], 2)
     pass_on(2, [z_peer(2), z_peer(NZ - 2)])
@@ -241,7 +260,16 @@
         acc2[1] += own[:3 * CH]
         acc2[2 * half] += own[3 * CH:]
 
-        receive(ok, cs.at[1, pl.ds(24 * half, 8)], c_recv.at[half])
+        far = jnp.logical_or(jnp.logical_and(half == 1, seam_down), jnp.logical_and(half == 0, seam_up))
+        edge = 24 * half
+
+        @pl.when(far)
+        def _():
+            arrived(cs.at[1, pl.ds(edge, 4)], c_recv.at[half])
+            for n in range(2):
+                arrived(cs.at[1, pl.ds(edge + 4 + 2 * n, 2)], w_recv.at[n])
+
+        pl.when(jnp.logical_not(far))(lambda: receive(ok, cs.at[1, pl.ds(edge, 8)], c_recv.at[half]))
         for k in range(8):
             c_row(3 * half, k)
         beyond = [stack(taps(cs, [24 * half + k])) for k in range(8)]
@@ -279,6 +307,36 @@
     for start, _ in g_out[2:]:
         start()
 
+    receive(there(-1, 0), gs.at[1, pl.ds(0, 4)], g_recv.at[6])
+    receive(there(1, 0), gs.at[1, pl.ds(20, 4)], g_recv.at[7])
+    for side, (ds, into) in enumerate(((-1, gleft), (1, gright))):
+        receive(there(0, ds), into.at[1], g_recv.at[side])
+        receive(there(-1, ds), into.at[0], g_recv.at[2 + side])
+        receive(there(1, ds), into.at[2], g_recv.at[4 + side])
+
+    def g_row(blk, e, at):
+        x = gs[1, e]
+        gs[2, e] = shift_right(x, gleft[blk], at, 4)
+        gs[0, e] = shift_left(x, gright[blk], at, 4)
+
+    for k in range(16):
+        g_row(1, 4 + k, 4 * k)
+    for k in range(4):
+        g_row(0, k, 4 * (12 + k))
+        g_row(2, 20 + k, 4 * k)
+
+    @pl.loop(0, TR // 4)
+    def _(g):
+        for k in range(4):
+            r = 4 * g + k
+            back = dot(w1t[...], stack(taps(gs, [r + 8, r + 4, r])))
+            out = gs[1, r + 4].astype(F32) + jnp.where(xf[r].astype(F32) > 0, back, 0.0)
+            xf[r] = out.astype(BF)
+
+    raw_f[...] = jnp.swapaxes(xf[...], 0, 1)
+    write_gf = pltpu.make_async_copy(raw_f, gf_ref, out_sem.at[0])
+    write_gf.start()
+
     mine = jnp.int32(0)
     is_owner = place < 0
     for j, owner in enumerate(OWNERS):
@@ -306,36 +364,6 @@
         for k in Z_STEPS:
             b_copy(k).start()
 
-    receive(there(-1, 0), gs.at[1, pl.ds(0, 4)], g_recv.at[6])
-    receive(there(1, 0), gs.at[1, pl.ds(20, 4)], g_recv.at[7])
-    for side, (ds, into) in enumerate(((-1, gleft), (1, gright))):
-        receive(there(0, ds), into.at[1], g_recv.at[side])
-        receive(there(-1, ds), into.at[0], g_recv.at[2 + side])
-        receive(there(1, ds), into.at[2], g_recv.at[4 + side])
-
-    def g_row(blk, e, at):
-        x = gs[1, e]
-        gs[2, e] = shift_right(x, gleft[blk], at, 4)
-        gs[0, e] = shift_left(x, gright[blk], at, 4)
-
-    for k in range(16):
-        g_row(1, 4 + k, 4 * k)
-    for k in range(4):
-        g_row(0, k, 4 * (12 + k))
-        g_row(2, 20 + k, 4 * k)
-
-    @pl.loop(0, TR // 4)
-    def _(g):
-        for k in range(4):
-            r = 4 * g + k
-            back = dot(w1t[...], stack(taps(gs, [r + 8, r + 4, r])))
-            out = gs[1, r + 4].astype(F32) + jnp.where(xf[r].astype(F32) > 0, back, 0.0)
-            xf[r] = out.astype(BF)
-
-    raw_f[...] = jnp.swapaxes(xf[...], 0, 1)
-    write_gf = pltpu.make_async_copy(raw_f, gf_ref, out_sem.at[0])
-    write_gf.start()
-
     @pl.when(is_owner)
     def _():
         full = rb[0].astype(F32)
@@ -346,7 +374,7 @@
         for n in range(PLANE - 1):
             o_copy(n).start()
 
-    for _, sent in f_out + p_out + c_out + g_out:
+    for _, sent in f_out + p_out + c_out + g_out + relay_out + [out for _, out in relay_on]:
         sent()
     for j in range(NCHUNK):
         pl.when(place != OWNERS[j])(lambda j=j: a_copy(j).wait_send())
@@ -421,6 +449,7 @@
             dma((2,)), dma((2,)), dma((2,)), dma((2,)), dma((6,)), dma((6,)), dma((8,)), dma((8,)),
             dma((NCHUNK,)), dma, dma((NZ - 1,)), dma((NZ - 1,)), dma((PLANE - 1,)), dma((NCHUNK,)),
             pltpu.SemaphoreType.REGULAR((3,)), dma((2,)),
+            buf(2, CH, TC), dma((2,)), dma, dma, dma((2,)),
         ],
         compiler_params=pltpu.CompilerParams(
             collective_id=0, has_side_effects=True, vmem_limit_bytes=60 << 20),

time: 46.3 us -> 44.5 us (0.961)
  Pallas kernels: 45.6 us -> 43.8 us
    pallas_call x1, Pallas kernels: 43.5 us -> 41.7 us  [shards(): pl.pallas_call(lambda *refs: kernel(scale, *refs), out_shape=(jax.ShapeDt...]
where the time goes in v4:
time: 44.5 us; the launch traced here: 44.4 us
  Pallas kernels  43.8 us (98%)
  between operations  0.64 us (1%)
    pallas_call x1, Pallas kernels, shards(): pl.pallas_call(lambda *refs: kernel(scale, *refs), out_shape=(jax.ShapeDt...  41.7 us
    pallas_call x1, Pallas kernels, shards(): pl.pallas_call(finish, out_shape=(jax.ShapeDtypeStruct((CH, TR, TC), BF),...  2.1 us

profile of v4, /device:TPU:1, one launch (start us, length us, event | category | flops | bytes accessed | tf_op | source)
XLA Modules:
  0.0 44.4 jit_solution(16107839304685889326)
XLA Ops:
  0.6 41.7 %dilated_backward.1 = (bf16[64,16,256]{2,1,0:T(8,128)(2,1)}, bf16[576,128]{1,0:T(8,128)(2,1)}) custom-call(bf16[64,16,256]{2,1,0:T(8,128)(2,1)} %refs_0_.1, bf16[64,16,256]{2,1,0:T(8,128)(2,1)} %refs_1_.1, bf16[9,64,64]{2,1,0:T(8,128)(2,1)} %refs_2_.1, bf16[9,64,64]{2,1,0:T(8,128)(2,1)} %refs_3_.1), custom_call_target="tpu_custom_call" | custom-call | tf_op jit(solution)/shard_map/dilated_backward/pallas_call | solution.py:433
  42.3 2.1 %finish.1 = (bf16[64,16,256]{2,1,0:T(8,128)(2,1)}, f32[9,64,64]{2,1,0:T(8,128)}, f32[9,64,64]{2,1,0:T(8,128)}) custom-call(bf16[64,16,256]{2,1,0:T(8,128)(2,1)} %get-tuple-element.5.gf_hbm, bf16[576,128]{1,0:T(8,128)(2,1)} %get-tuple-element.6.gr_hbm), custom_call_target="tpu_custom_call" | custom-call | tf_op jit(solution)/shard_map/finish/pallas_call | solution.py:459

commit v5 on v4

--- a/solution.py
+++ b/solution.py
@@ -17,19 +17,16 @@
 NZ = LONG // PLANE * SHORT
 CHUNK = 32
 NCHUNK = K // CHUNK
-OWNERS = (8, 9, 22, 23, 2, 28, 16, 17, 4, 5, 14, 15, 26, 27, 24, 25, 6, 7)
+OWNERS = (10, 21, 12, 19, 2, 9, 22, 29, 4, 13, 15, 16, 27, 18, 6, 7, 24, 25)
 
 NEAR = ((-1, 0), (1, 0), (0, -1), (0, 1), (-1, -1), (-1, 1), (1, -1), (1, 1))
 
 
-def ring_distance(a, n):
-    return min(a % n, -a % n)
-
-
-PLANE_STEPS = sorted(
-    [(y, x, c) for y in range(4) for x in range(4) for c in range(2) if (y, x, c) != (0, 0, 0)],
-    key=lambda t: -(ring_distance(t[0], 4) + ring_distance(t[1], 4)))
-Z_STEPS = sorted(range(1, NZ), key=lambda k: -ring_distance(k, NZ))
+PLANE_FLIPS = sorted(
+    range(1, PLANE), key=lambda m: -((2 if m // 2 % 4 == 2 else min(m // 2 % 4, 1)) + (2 if m // 8 == 2 else min(m // 8, 1))))
+ROW_FLIPS = [m for m in PLANE_FLIPS if m < 8]
+COLUMN_FLIPS = [m for m in PLANE_FLIPS if m % 8 == 0]
+Z_FLIPS = (4, 5, 3, 7, 6, 2, 1)
 
 
 def nt_dot(a, b):
@@ -76,19 +73,30 @@
             ok = here if ok is None else jnp.logical_and(ok, here)
         return ok
 
-    def plane_peer(step):
-        y, x, c = step
-        py = lax.rem(lax.div(place, 8) + y, 4)
-        px = lax.rem(lax.div(place, 2) + x, 4)
-        return base + py * 8 + px * 2 + lax.rem(core + c, 2), s
+    def flips(at, bits):
+        return [b - 2 * b * lax.rem(lax.div(at, b), 2) for b in bits]
+
+    place_flips = flips(place, (1, 2, 4, 8, 16))
+    short_flips = flips(s, (1, 2))
+    group_flip = PLANE - 2 * PLANE * lax.div(l, PLANE)
+
+    def flipped(at, steps, m):
+        for n, step in enumerate(steps):
+            if m >> n & 1:
+                at = at + step
+        return at
+
+    def plane_peer(m):
+        return flipped(l, place_flips, m), s
+
+    def z_flip(m):
+        return (l + group_flip if m & 4 else l), flipped(s, short_flips, m & 3)
 
     def z_peer(k):
         other = lax.rem(z + k, NZ)
         return lax.div(other, SHORT) * PLANE + place, lax.rem(other, SHORT)
 
-    row_steps = [step for step in PLANE_STEPS if step[0] == 0]
-    column_steps = [step for step in PLANE_STEPS if step[1:] == (0, 0)]
-    first = [plane_peer(step) for step in row_steps + column_steps] + [z_peer(1), z_peer(NZ - 1)]
+    first = [plane_peer(m) for m in ROW_FLIPS + COLUMN_FLIPS] + [z_peer(1), z_peer(NZ - 1)]
     greetings = jnp.int32(len(first))
     for dl, ds in NEAR:
         pl.when(there(dl, ds))(lambda dl=dl, ds=ds: greet((l + dl, s + ds)))
@@ -166,7 +174,7 @@
     pl.semaphore_wait(barrier, greetings)
     for start, _ in relay_out + f_out + p_out + c_out:
         start()
-    pass_on(0, [plane_peer(step) for step in row_steps])
+    pass_on(0, [plane_peer(m) for m in ROW_FLIPS])
     pass_on(1, [z_peer(1), z_peer(NZ - 1)])
 
     fetch[2].wait()
@@ -210,7 +218,7 @@
     for here, (start, _) in relay_on:
         pl.when(here)(lambda: arrived(relay, r_recv))
         start()
-    pl.semaphore_wait(ready.at[0], len(row_steps))
+    pl.semaphore_wait(ready.at[0], len(ROW_FLIPS))
     pl.semaphore_wait(ready.at[1], 2)
     pass_on(2, [z_peer(2), z_peer(NZ - 2)])
 
@@ -288,7 +296,7 @@
 
     def a_copy(j):
         owner = OWNERS[j]
-        slot = lax.rem(place - owner + PLANE - 1, PLANE)
+        slot = place - (place > owner).astype(jnp.int32)
         return pltpu.make_async_remote_copy(
             src_ref=gb.at[pl.ds(CHUNK * j, CHUNK)], dst_ref=ra.at[slot],
             send_sem=a_send.at[j], recv_sem=a_recv,
@@ -334,7 +342,7 @@
             xf[r] = out.astype(BF)
 
     raw_f[...] = jnp.swapaxes(xf[...], 0, 1)
-    write_gf = pltpu.make_async_copy(raw_f, gf_ref, out_sem.at[0])
+    write_gf = pltpu.make_async_copy(raw_f, gf_ref, out_sem)
     write_gf.start()
 
     mine = jnp.int32(0)
@@ -347,12 +355,12 @@
     def b_copy(k):
         return pltpu.make_async_remote_copy(
             src_ref=rb.at[0], dst_ref=rb.at[k], send_sem=b_send.at[k - 1], recv_sem=b_recv.at[k - 1],
-            device_id=z_peer(k), device_id_type=MESH)
+            device_id=z_flip(k), device_id_type=MESH)
 
     def o_copy(n):
         return pltpu.make_async_remote_copy(
             src_ref=fin.at[my_rows], dst_ref=fin.at[my_rows], send_sem=o_send.at[n],
-            recv_sem=o_recv.at[mine], device_id=plane_peer(PLANE_STEPS[n]), device_id_type=MESH)
+            recv_sem=o_recv, device_id=plane_peer(PLANE_FLIPS[n]), device_id_type=MESH)
 
     @pl.when(is_owner)
     def _():
@@ -361,13 +369,13 @@
         for i in range(PLANE - 1):
             total += ra[i].astype(F32)
         rb[0] = total.astype(BF)
-        for k in Z_STEPS:
+        for k in Z_FLIPS:
             b_copy(k).start()
 
     @pl.when(is_owner)
     def _():
         full = rb[0].astype(F32)
-        for k in reversed(Z_STEPS):
+        for k in reversed(Z_FLIPS):
             b_copy(k).wait_recv()
             full += rb[k].astype(F32)
         fin[my_rows, :] = (full * scale).astype(BF)
@@ -379,34 +387,28 @@
     for j in range(NCHUNK):
         pl.when(place != OWNERS[j])(lambda j=j: a_copy(j).wait_send())
 
-    for j in range(NCHUNK):
-        pl.when(place != OWNERS[j])(
-            lambda j=j: arrived(fin.at[pl.ds(CHUNK * j, CHUNK)], o_recv.at[j]))
-    write_gr = pltpu.make_async_copy(fin, gr_ref, out_sem.at[1])
-    write_gr.start()
+    pl.when(is_owner)(lambda: arrived(fin.at[pl.ds(0, K - CHUNK)], o_recv))
+    pl.when(jnp.logical_not(is_owner))(lambda: arrived(fin, o_recv))
+    gr_ref[...] = fin[...]
 
     @pl.when(is_owner)
     def _():
-        for k in Z_STEPS:
+        for k in Z_FLIPS:
             b_copy(k).wait_send()
         for n in range(PLANE - 1):
             o_copy(n).wait_send()
 
     write_gf.wait()
-    write_gr.wait()
-
-
-def finish(gf_hbm, gr_hbm, out_hbm, first_hbm, second_hbm, gf, gr, first, second, load, store):
+
+
+def finish(gf_hbm, gr, out_hbm, first_hbm, second_hbm, gf, first, second, load, store):
     parts = 4
     step = CH // parts
-    read = pltpu.make_async_copy(gr_hbm, gr, load.at[parts])
-    read.start()
     blocks = [pl.ds(i * step, step) for i in range(parts)]
     loads = [pltpu.make_async_copy(gf_hbm.at[b], gf.at[b], load.at[i]) for i, b in enumerate(blocks)]
     stores = [pltpu.make_async_copy(gf.at[b], out_hbm.at[b], store.at[i]) for i, b in enumerate(blocks)]
     for copy in loads:
         copy.start()
-    read.wait()
     both = gr[...].astype(F32).reshape(9, CH, 2 * CH)
     first[...] = both[:, :, CH:]
     second[...] = both[:, :, :CH]
@@ -434,7 +436,7 @@
         lambda *refs: kernel(scale, *refs),
         out_shape=(jax.ShapeDtypeStruct((CH, TR, TC), BF), jax.ShapeDtypeStruct((K, 2 * CH), BF)),
         in_specs=[hbm] * 4,
-        out_specs=(hbm, hbm),
+        out_specs=(hbm, vmem),
         scratch_shapes=[
             buf(CH, TR, TC), buf(CH, TR, TC), buf(9, CH, CH), buf(9, CH, CH),
             buf(TR, CH, TC), buf(TR, CH, TC),
@@ -447,23 +449,23 @@
             buf(PLANE - 1, CHUNK, 2 * CH), buf(NZ, CHUNK, 2 * CH), buf(K, 2 * CH),
             dma((4,)),
             dma((2,)), dma((2,)), dma((2,)), dma((2,)), dma((6,)), dma((6,)), dma((8,)), dma((8,)),
-            dma((NCHUNK,)), dma, dma((NZ - 1,)), dma((NZ - 1,)), dma((PLANE - 1,)), dma((NCHUNK,)),
-            pltpu.SemaphoreType.REGULAR((3,)), dma((2,)),
+            dma((NCHUNK,)), dma, dma((NZ - 1,)), dma((NZ - 1,)), dma((PLANE - 1,)), dma,
+            pltpu.SemaphoreType.REGULAR((3,)), dma,
             buf(2, CH, TC), dma((2,)), dma, dma, dma((2,)),
         ],
         compiler_params=pltpu.CompilerParams(
-            collective_id=0, has_side_effects=True, vmem_limit_bytes=60 << 20),
+            collective_id=0, has_side_effects=True, vmem_limit_bytes=215 << 18),
         name="dilated_backward",
     )(field, cotangent, first_filter, second_filter)
     taps = jax.ShapeDtypeStruct((9, CH, CH), F32)
     return pl.pallas_call(
         finish,
         out_shape=(jax.ShapeDtypeStruct((CH, TR, TC), BF), taps, taps),
-        in_specs=[hbm, hbm],
+        in_specs=[hbm, vmem],
         out_specs=(hbm, hbm, hbm),
         scratch_shapes=[
-            buf(CH, TR, TC), buf(K, 2 * CH), buf(9, CH, CH, dtype=F32), buf(9, CH, CH, dtype=F32), dma((5,)), dma((6,))],
-        compiler_params=pltpu.CompilerParams(vmem_limit_bytes=60 << 20),
+            buf(CH, TR, TC), buf(9, CH, CH, dtype=F32), buf(9, CH, CH, dtype=F32), dma((4,)), dma((6,))],
+        compiler_params=pltpu.CompilerParams(vmem_limit_bytes=215 << 18),
         name="finish",
     )(gf, gr)
 

time: 44.5 us -> 43.5 us (0.978)
  Pallas kernels: 43.8 us -> 42.7 us
    pallas_call x1, Pallas kernels: 41.7 us -> 40.7 us  [shards(): pl.pallas_call(lambda *refs: kernel(scale, *refs), out_shape=(jax.ShapeDt...]
where the time goes in v5:
time: 43.5 us; the launch traced here: 43.4 us
  Pallas kernels  42.7 us (98%)
  between operations  0.64 us (1%)
    pallas_call x1, Pallas kernels, shards(): pl.pallas_call(lambda *refs: kernel(scale, *refs), out_shape=(jax.ShapeDt...  40.7 us
    pallas_call x1, Pallas kernels, shards(): pl.pallas_call(finish, out_shape=(jax.ShapeDtypeStruct((CH, TR, TC), BF),...  2.07 us

profile of v5, /device:TPU:1, one launch (start us, length us, event | category | flops | bytes accessed | tf_op | source)
XLA Modules:
  0.0 43.4 jit_solution(10062868159226879697)
XLA Ops:
  0.6 40.7 %dilated_backward.1 = (bf16[64,16,256]{2,1,0:T(8,128)(2,1)}, bf16[576,128]{1,0:T(8,128)(2,1)S(1)}) custom-call(bf16[64,16,256]{2,1,0:T(8,128)(2,1)} %refs_0_.1, bf16[64,16,256]{2,1,0:T(8,128)(2,1)} %refs_1_.1, bf16[9,64,64]{2,1,0:T(8,128)(2,1)} %refs_2_.1, bf16[9,64,64]{2,1,0:T(8,128)(2,1)} %refs_3_.1), custom_call_target="tpu_custom_call" | custom-call | tf_op jit(solution)/shard_map/dilated_backward/pallas_call | solution.py:435
  41.3 2.1 %finish.1 = (bf16[64,16,256]{2,1,0:T(8,128)(2,1)}, f32[9,64,64]{2,1,0:T(8,128)}, f32[9,64,64]{2,1,0:T(8,128)}) custom-call(bf16[64,16,256]{2,1,0:T(8,128)(2,1)} %get-tuple-element.5.gf_hbm, bf16[576,128]{1,0:T(8,128)(2,1)S(1)} %get-tuple-element.6.gr), custom_call_target="tpu_custom_call" | custom-call | tf_op jit(solution)/shard_map/finish/pallas_call | solution.py:461

commit v6 on v5

--- a/solution.py
+++ b/solution.py
@@ -41,11 +41,11 @@
     pltpu.make_async_copy(ref, ref, sem).wait()
 
 
-def kernel(scale, field_hbm, cot_hbm, w1_hbm, w2_hbm, gf_ref, gr_ref,
+def kernel(scale, field_hbm, cot_hbm, w1_hbm, w2_hbm, both_ref,
            raw_f, raw_c, raw_w1, raw_w2, xf, a2, fs, cs, gs, ps, pleft, pright, gps, gleft, gright,
            w1c, w1t, w2own, w2halo, up_own, acc2, acc1, gb, ra, rb, fin, in_sem,
            f_send, f_recv, c_send, c_recv, p_send, p_recv, g_send, g_recv,
-           a_send, a_recv, b_send, b_recv, o_send, o_recv, ready, out_sem,
+           a_send, a_recv, b_send, b_recv, o_send, o_recv, ready,
            relay, r_send, r_recv, w_send, w_recv):
     l = lax.axis_index("long")
     s = lax.axis_index("short")
@@ -341,9 +341,7 @@
             out = gs[1, r + 4].astype(F32) + jnp.where(xf[r].astype(F32) > 0, back, 0.0)
             xf[r] = out.astype(BF)
 
-    raw_f[...] = jnp.swapaxes(xf[...], 0, 1)
-    write_gf = pltpu.make_async_copy(raw_f, gf_ref, out_sem)
-    write_gf.start()
+    both_ref[:CH] = jnp.swapaxes(xf[...], 0, 1)
 
     mine = jnp.int32(0)
     is_owner = place < 0
@@ -389,7 +387,9 @@
 
     pl.when(is_owner)(lambda: arrived(fin.at[pl.ds(0, K - CHUNK)], o_recv))
     pl.when(jnp.logical_not(is_owner))(lambda: arrived(fin, o_recv))
-    gr_ref[...] = fin[...]
+    for j in range(NCHUNK):
+        both_ref[CH + j] = jnp.concatenate(
+            [fin[CHUNK * j:CHUNK * j + TR, :], fin[CHUNK * j + TR:CHUNK * (j + 1), :]], axis=1)
 
     @pl.when(is_owner)
     def _():
@@ -398,27 +398,19 @@
         for n in range(PLANE - 1):
             o_copy(n).wait_send()
 
-    write_gf.wait()
-
-
-def finish(gf_hbm, gr, out_hbm, first_hbm, second_hbm, gf, first, second, load, store):
-    parts = 4
-    step = CH // parts
-    blocks = [pl.ds(i * step, step) for i in range(parts)]
-    loads = [pltpu.make_async_copy(gf_hbm.at[b], gf.at[b], load.at[i]) for i, b in enumerate(blocks)]
-    stores = [pltpu.make_async_copy(gf.at[b], out_hbm.at[b], store.at[i]) for i, b in enumerate(blocks)]
-    for copy in loads:
-        copy.start()
-    both = gr[...].astype(F32).reshape(9, CH, 2 * CH)
-    first[...] = both[:, :, CH:]
-    second[...] = both[:, :, :CH]
-    stores.append(pltpu.make_async_copy(first, first_hbm, store.at[parts]))
-    stores.append(pltpu.make_async_copy(second, second_hbm, store.at[parts + 1]))
-    stores[parts].start()
-    stores[parts + 1].start()
-    for i in range(parts):
-        loads[i].wait()
-        stores[i].start()
+
+def finish(both, out_hbm, first_hbm, second_hbm, first, second, store):
+    stores = [pltpu.make_async_copy(src, dst, store.at[i]) for i, (src, dst) in enumerate(
+        ((both.at[pl.ds(0, CH)], out_hbm), (first, first_hbm), (second, second_hbm)))]
+    stores[0].start()
+    for t in range(9):
+        for q in range(CH // TR):
+            rows, lanes = slice(TR * q, TR * (q + 1)), slice(2 * CH * (q % 2), 2 * CH * (q % 2 + 1))
+            part = both[CH + 2 * t + q // 2, :, lanes].astype(F32)
+            first[t, rows] = part[:, CH:]
+            second[t, rows] = part[:, :CH]
+    stores[1].start()
+    stores[2].start()
     for copy in stores:
         copy.wait()
 
@@ -432,11 +424,11 @@
     def buf(*shape, dtype=BF):
         return pltpu.VMEM(shape, dtype)
 
-    gf, gr = pl.pallas_call(
+    both = pl.pallas_call(
         lambda *refs: kernel(scale, *refs),
-        out_shape=(jax.ShapeDtypeStruct((CH, TR, TC), BF), jax.ShapeDtypeStruct((K, 2 * CH), BF)),
+        out_shape=pltpu.VMEM((CH + NCHUNK, TR, TC), BF),
         in_specs=[hbm] * 4,
-        out_specs=(hbm, vmem),
+        out_specs=vmem,
         scratch_shapes=[
             buf(CH, TR, TC), buf(CH, TR, TC), buf(9, CH, CH), buf(9, CH, CH),
             buf(TR, CH, TC), buf(TR, CH, TC),
@@ -450,24 +442,24 @@
             dma((4,)),
             dma((2,)), dma((2,)), dma((2,)), dma((2,)), dma((6,)), dma((6,)), dma((8,)), dma((8,)),
             dma((NCHUNK,)), dma, dma((NZ - 1,)), dma((NZ - 1,)), dma((PLANE - 1,)), dma,
-            pltpu.SemaphoreType.REGULAR((3,)), dma,
+            pltpu.SemaphoreType.REGULAR((3,)),
             buf(2, CH, TC), dma((2,)), dma, dma, dma((2,)),
         ],
         compiler_params=pltpu.CompilerParams(
-            collective_id=0, has_side_effects=True, vmem_limit_bytes=215 << 18),
+            collective_id=0, has_side_effects=True, vmem_limit_bytes=60 << 20),
         name="dilated_backward",
     )(field, cotangent, first_filter, second_filter)
     taps = jax.ShapeDtypeStruct((9, CH, CH), F32)
     return pl.pallas_call(
         finish,
         out_shape=(jax.ShapeDtypeStruct((CH, TR, TC), BF), taps, taps),
-        in_specs=[hbm, vmem],
+        in_specs=[vmem],
         out_specs=(hbm, hbm, hbm),
         scratch_shapes=[
-            buf(CH, TR, TC), buf(9, CH, CH, dtype=F32), buf(9, CH, CH, dtype=F32), dma((4,)), dma((6,))],
-        compiler_params=pltpu.CompilerParams(vmem_limit_bytes=215 << 18),
+            buf(9, CH, CH, dtype=F32), buf(9, CH, CH, dtype=F32), dma((3,))],
+        compiler_params=pltpu.CompilerParams(vmem_limit_bytes=16 << 20),
         name="finish",
-    )(gf, gr)
+    )(both)
 
 
 def solution(mesh):

time: 43.5 us -> 42.4 us (0.975)
  Pallas kernels: 42.7 us -> 41.6 us
    pallas_call x1, Pallas kernels: 2.07 us -> 1.01 us  [shards(): pl.pallas_call(finish, out_shape=(jax.ShapeDtypeStruct((CH, TR, TC), BF),...]
where the time goes in v6:
time: 42.4 us; the launch traced here: 42.3 us
  Pallas kernels  41.6 us (98%)
  between operations  0.64 us (2%)
    pallas_call x1, Pallas kernels, shards(): pl.pallas_call(lambda *refs: kernel(scale, *refs), out_shape=pltpu.VMEM((...  40.6 us
    pallas_call x1, Pallas kernels, shards(): pl.pallas_call(finish, out_shape=(jax.ShapeDtypeStruct((CH, TR, TC), BF),...  1.01 us

profile of v6, /device:TPU:1, one launch (start us, length us, event | category | flops | bytes accessed | tf_op | source)
XLA Modules:
  0.0 42.3 jit_solution(18385885538925038599)
XLA Ops:
  0.6 40.6 %dilated_backward.1.both = bf16[82,16,256]{2,1,0:T(8,128)(2,1)S(1)} custom-call(bf16[64,16,256]{2,1,0:T(8,128)(2,1)} %refs_0_.1, bf16[64,16,256]{2,1,0:T(8,128)(2,1)} %refs_1_.1, bf16[9,64,64]{2,1,0:T(8,128)(2,1)} %refs_2_.1, bf16[9,64,64]{2,1,0:T(8,128)(2,1)} %refs_3_.1), custom_call_target="tpu_custom_call" | custom-call | tf_op jit(solution)/shard_map/dilated_backward/pallas_call | solution.py:427
  41.3 1.0 %finish.1 = (bf16[64,16,256]{2,1,0:T(8,128)(2,1)}, f32[9,64,64]{2,1,0:T(8,128)}, f32[9,64,64]{2,1,0:T(8,128)}) custom-call(bf16[82,16,256]{2,1,0:T(8,128)(2,1)S(1)} %dilated_backward.1.both), custom_call_target="tpu_custom_call" | custom-call | tf_op jit(solution)/shard_map/finish/pallas_call | solution.py:453

commit v7 on v6

--- a/solution.py
+++ b/solution.py
@@ -123,14 +123,16 @@
         def _():
             dst[...] = jnp.zeros(dst.shape, dst.dtype)
 
-    f_out = [message(-1, 0, fs.at[1, pl.ds(4, 4)], fs.at[1, pl.ds(20, 4)], f_send.at[0], f_recv.at[1]),
-             message(1, 0, fs.at[1, pl.ds(16, 4)], fs.at[1, pl.ds(0, 4)], f_send.at[1], f_recv.at[0])]
     seam_down = jnp.logical_and(place == PLANE - 1, l < LONG - 1)
     seam_up = jnp.logical_and(place == 0, l > 0)
     up, down = jnp.logical_and(l > 0, place != 0), jnp.logical_and(l < LONG - 1, place != PLANE - 1)
+    f_out = [message(-1, 0, fs.at[1, pl.ds(4, 4)], fs.at[1, pl.ds(20, 4)], f_send.at[0], f_recv.at[1], up),
+             message(1, 0, fs.at[1, pl.ds(16, 4)], fs.at[1, pl.ds(0, 4)], f_send.at[1], f_recv.at[0], down)]
+    f_far = [message(-1, 0, fs.at[1, pl.ds(4, 4)], fs.at[1, pl.ds(20, 4)], f_send.at[0], f_recv.at[1], seam_up),
+             message(1, 0, fs.at[1, pl.ds(16, 4)], fs.at[1, pl.ds(0, 4)], f_send.at[1], f_recv.at[0], seam_down)]
     c_out = [message(-1, 0, cs.at[1, pl.ds(8, 8)], cs.at[1, pl.ds(24, 8)], c_send.at[0], c_recv.at[1], up),
-             message(1, 0, cs.at[1, pl.ds(16, 8)], cs.at[1, pl.ds(0, 8)], c_send.at[1], c_recv.at[0], down),
-             message(-1, 0, cs.at[1, pl.ds(8, 4)], cs.at[1, pl.ds(24, 4)], c_send.at[0], c_recv.at[1], seam_up),
+             message(1, 0, cs.at[1, pl.ds(16, 8)], cs.at[1, pl.ds(0, 8)], c_send.at[1], c_recv.at[0], down)]
+    c_far = [message(-1, 0, cs.at[1, pl.ds(8, 4)], cs.at[1, pl.ds(24, 4)], c_send.at[0], c_recv.at[1], seam_up),
              message(1, 0, cs.at[1, pl.ds(16, 4)], cs.at[1, pl.ds(0, 4)], c_send.at[1], c_recv.at[0], seam_down)]
     relay_out, relay_on = [], []
     for n, hop in enumerate((2, 8)):
@@ -172,7 +174,7 @@
             ps[side, half] = jnp.concatenate(pieces, axis=1)
 
     pl.semaphore_wait(barrier, greetings)
-    for start, _ in relay_out + f_out + p_out + c_out:
+    for start, _ in f_far + p_out + relay_out + f_out + c_out:
         start()
     pass_on(0, [plane_peer(m) for m in ROW_FLIPS])
     pass_on(1, [z_peer(1), z_peer(NZ - 1)])
@@ -186,6 +188,11 @@
     for half in range(2):
         w2own[half] = jnp.concatenate([taps_of[1], taps_of[2 * half]], axis=1)
         w2halo[half] = taps_of[2 - 2 * half]
+
+    for _, sent in f_far:
+        sent()
+    for start, _ in c_far:
+        start()
 
     acc2[...] = jnp.zeros_like(acc2)
     acc1[...] = jnp.zeros_like(acc1)
@@ -380,7 +387,7 @@
         for n in range(PLANE - 1):
             o_copy(n).start()
 
-    for _, sent in f_out + p_out + c_out + g_out + relay_out + [out for _, out in relay_on]:
+    for _, sent in f_out + p_out + c_out + c_far + g_out + relay_out + [out for _, out in relay_on]:
         sent()
     for j in range(NCHUNK):
         pl.when(place != OWNERS[j])(lambda j=j: a_copy(j).wait_send())

time: 42.4 us -> 42.4 us (level)
  no operation moved by 1% of the time
where the time goes in v7:
time: 42.4 us; the launch traced here: 42.3 us
  Pallas kernels  41.7 us (98%)
  between operations  0.64 us (2%)
    pallas_call x1, Pallas kernels, shards(): pl.pallas_call(lambda *refs: kernel(scale, *refs), out_shape=pltpu.VMEM((...  40.6 us
    pallas_call x1, Pallas kernels, shards(): pl.pallas_call(finish, out_shape=(jax.ShapeDtypeStruct((CH, TR, TC), BF),...  1.01 us

profile of v7, /device:TPU:1, one launch (start us, length us, event | category | flops | bytes accessed | tf_op | source)
XLA Modules:
  0.0 42.3 jit_solution(9821797493741720335)
XLA Ops:
  0.6 40.6 %dilated_backward.1.both = bf16[82,16,256]{2,1,0:T(8,128)(2,1)S(1)} custom-call(bf16[64,16,256]{2,1,0:T(8,128)(2,1)} %refs_0_.1, bf16[64,16,256]{2,1,0:T(8,128)(2,1)} %refs_1_.1, bf16[9,64,64]{2,1,0:T(8,128)(2,1)} %refs_2_.1, bf16[9,64,64]{2,1,0:T(8,128)(2,1)} %refs_3_.1), custom_call_target="tpu_custom_call" | custom-call | tf_op jit(solution)/shard_map/dilated_backward/pallas_call | solution.py:434
  41.3 1.0 %finish.1 = (bf16[64,16,256]{2,1,0:T(8,128)(2,1)}, f32[9,64,64]{2,1,0:T(8,128)}, f32[9,64,64]{2,1,0:T(8,128)}) custom-call(bf16[82,16,256]{2,1,0:T(8,128)(2,1)S(1)} %dilated_backward.1.both), custom_call_target="tpu_custom_call" | custom-call | tf_op jit(solution)/shard_map/finish/pallas_call | solution.py:460

commit v8 on v7

--- a/solution.py
+++ b/solution.py
@@ -297,10 +297,6 @@
             jnp.concatenate([gs[1, r + 4] for r in rows], axis=1),
             jnp.concatenate([stack(taps(fs, [r, r + 4, r + 8])) for r in rows], axis=1))
 
-    for t in range(9):
-        gb[CH * t:CH * (t + 1), :] = jnp.concatenate(
-            [acc2[t // 3, CH * (t % 3):CH * (t % 3 + 1), :], acc1[:, CH * t:CH * (t + 1)]], axis=1).astype(BF)
-
     def a_copy(j):
         owner = OWNERS[j]
         slot = place - (place > owner).astype(jnp.int32)
@@ -309,8 +305,11 @@
             send_sem=a_send.at[j], recv_sem=a_recv,
             device_id=(base + owner, s), device_id_type=MESH)
 
-    for j in range(NCHUNK):
-        pl.when(place != OWNERS[j])(lambda j=j: a_copy(j).start())
+    for t in range(9):
+        gb[CH * t:CH * (t + 1), :] = jnp.concatenate(
+            [acc2[t // 3, CH * (t % 3):CH * (t % 3 + 1), :], acc1[:, CH * t:CH * (t + 1)]], axis=1).astype(BF)
+        for j in range(CH // CHUNK * t, CH // CHUNK * (t + 1)):
+            pl.when(place != OWNERS[j])(lambda j=j: a_copy(j).start())
     pl.semaphore_wait(ready.at[2], 2)
 
     for start, _ in g_out[:2]:

time: 42.4 us -> 42.5 us (level)
  no operation moved by 1% of the time
where the time goes in v8:
time: 42.5 us; the launch traced here: 42.4 us
  Pallas kernels  41.8 us (98%)
  between operations  0.64 us (2%)
    pallas_call x1, Pallas kernels, shards(): pl.pallas_call(lambda *refs: kernel(scale, *refs), out_shape=pltpu.VMEM((...  40.8 us
    pallas_call x1, Pallas kernels, shards(): pl.pallas_call(finish, out_shape=(jax.ShapeDtypeStruct((CH, TR, TC), BF),...  1.01 us

profile of v8, /device:TPU:1, one launch (start us, length us, event | category | flops | bytes accessed | tf_op | source)
XLA Modules:
  0.0 42.4 jit_solution(13507025163246270348)
XLA Ops:
  0.6 40.8 %dilated_backward.1.both = bf16[82,16,256]{2,1,0:T(8,128)(2,1)S(1)} custom-call(bf16[64,16,256]{2,1,0:T(8,128)(2,1)} %refs_0_.1, bf16[64,16,256]{2,1,0:T(8,128)(2,1)} %refs_1_.1, bf16[9,64,64]{2,1,0:T(8,128)(2,1)} %refs_2_.1, bf16[9,64,64]{2,1,0:T(8,128)(2,1)} %refs_3_.1), custom_call_target="tpu_custom_call" | custom-call | tf_op jit(solution)/shard_map/dilated_backward/pallas_call | solution.py:433
  41.4 1.0 %finish.1 = (bf16[64,16,256]{2,1,0:T(8,128)(2,1)}, f32[9,64,64]{2,1,0:T(8,128)}, f32[9,64,64]{2,1,0:T(8,128)}) custom-call(bf16[82,16,256]{2,1,0:T(8,128)(2,1)S(1)} %dilated_backward.1.both), custom_call_target="tpu_custom_call" | custom-call | tf_op jit(solution)/shard_map/finish/pallas_call | solution.py:459

commit v9 on v8

--- a/solution.py
+++ b/solution.py
@@ -17,7 +17,7 @@
 NZ = LONG // PLANE * SHORT
 CHUNK = 32
 NCHUNK = K // CHUNK
-OWNERS = (10, 21, 12, 19, 2, 9, 22, 29, 4, 13, 15, 16, 27, 18, 6, 7, 24, 25)
+OWNERS = (10, 21, 12, 19, 3, 9, 22, 28, 4, 13, 15, 16, 27, 18, 6, 7, 24, 25)
 
 NEAR = ((-1, 0), (1, 0), (0, -1), (0, 1), (-1, -1), (-1, 1), (1, -1), (1, 1))
 

time: 42.5 us -> 43 us (1.012)
  Pallas kernels: 41.8 us -> 42.3 us
    pallas_call x1, Pallas kernels: 40.8 us -> 41.3 us  [shards(): pl.pallas_call(lambda *refs: kernel(scale, *refs), out_shape=pltpu.VMEM((...]
where the time goes in v9:
time: 43 us; the launch traced here: 42.9 us
  Pallas kernels  42.3 us (98%)
  between operations  0.64 us (1%)
    pallas_call x1, Pallas kernels, shards(): pl.pallas_call(lambda *refs: kernel(scale, *refs), out_shape=pltpu.VMEM((...  41.3 us
    pallas_call x1, Pallas kernels, shards(): pl.pallas_call(finish, out_shape=(jax.ShapeDtypeStruct((CH, TR, TC), BF),...  1.01 us

profile of v9, /device:TPU:1, one launch (start us, length us, event | category | flops | bytes accessed | tf_op | source)
XLA Modules:
  0.0 42.9 jit_solution(1113499628964066875)
XLA Ops:
  0.6 41.3 %dilated_backward.1.both = bf16[82,16,256]{2,1,0:T(8,128)(2,1)S(1)} custom-call(bf16[64,16,256]{2,1,0:T(8,128)(2,1)} %refs_0_.1, bf16[64,16,256]{2,1,0:T(8,128)(2,1)} %refs_1_.1, bf16[9,64,64]{2,1,0:T(8,128)(2,1)} %refs_2_.1, bf16[9,64,64]{2,1,0:T(8,128)(2,1)} %refs_3_.1), custom_call_target="tpu_custom_call" | custom-call | tf_op jit(solution)/shard_map/dilated_backward/pallas_call | solution.py:433
  41.9 1.0 %finish.1 = (bf16[64,16,256]{2,1,0:T(8,128)(2,1)}, f32[9,64,64]{2,1,0:T(8,128)}, f32[9,64,64]{2,1,0:T(8,128)}) custom-call(bf16[82,16,256]{2,1,0:T(8,128)(2,1)S(1)} %dilated_backward.1.both), custom_call_target="tpu_custom_call" | custom-call | tf_op jit(solution)/shard_map/finish/pallas_call | solution.py:459
